TPU v7x, 32 devices: a whole 2x2x4 slice. The times are simulated.
32 devices in a mesh: dp: 16 (over z, y, core), seq: 2 (over x).
Axes of the slice: x: 2, y: 2, z: 4, core: 2. Of those that a mesh axis runs over, the one named last changes fastest.
Arguments:
- inputs: bfloat16 [16, 2048, 512], P('dp', 'seq'), may hold values from -6 to 6
- cotangent: bfloat16 [16, 2048, 512], P('dp', 'seq'), may hold values from -6 to 6
- neighbours: int32 [16, 2048, 4], P('dp', 'seq'), may hold values from 0 to 2047, as said below
- empty_rows: int32 [16, 2048], P('dp', 'seq'), may hold values 0 or 1
- first_gain: float32 [512], replicated, may hold values from 0.25 to 1.75
- query_weight: bfloat16 [512, 512], replicated, may hold values from -0.25 to 0.25
- key_weight: bfloat16 [512, 512], replicated, may hold values from -0.25 to 0.25
- value_weight: bfloat16 [512, 512], replicated, may hold values from -0.25 to 0.25
- gate_weight: bfloat16 [512, 8], replicated, may hold values from -0.25 to 0.25
- output_weight: bfloat16 [512, 512], replicated, may hold values from -1.5 to 1.5
- second_gain: float32 [512], replicated, may hold values from 0.25 to 1.75
- hidden_weight: bfloat16 [512, 2048], replicated, may hold values from -0.25 to 0.25
- return_weight: bfloat16 [2048, 512], replicated, may hold values from -0.125 to 0.125
Outputs:
- outputs: bfloat16 [16, 2048, 512], P('dp', 'seq')
- input_grad: bfloat16 [16, 2048, 512], P('dp', 'seq')
- first_gain_grad: float32 [512], replicated
- query_weight_grad: float32 [512, 512], replicated
- key_weight_grad: float32 [512, 512], replicated
- value_weight_grad: float32 [512, 512], replicated
- gate_weight_grad: float32 [512, 8], replicated
- output_weight_grad: float32 [512, 512], replicated
- second_gain_grad: float32 [512], replicated
- hidden_weight_grad: float32 [512, 2048], replicated
- return_weight_grad: float32 [2048, 512], replicated
Inputs may be any that keep to these rules, and one draw needn't show every extreme that they name: `neighbours`: positions within the token's own sequence; the sequence is cut into 2 shards of 1024 consecutive positions, and among the 4096 entries of the tokens of one shard, the positions of each shard are named exactly 2048 times.
All inputs are finite; a program needn't handle non-finite values. No bound on the sum of `empty_rows` on one device may be relied on, other than what follows from the above.
Results may differ from a plain program's by a relative error of at most 0.012.
Values may be sent and summed in bfloat16 or wider, within the bound.
No kernel may reach another device: no remote copies, remote signals or barrier semaphores. Data moves between devices by JAX's collectives and lax.ppermute only.
A program may use at most 320 MiB of HBM per device.

v0:
```python
import functools
import math

import jax
import jax.numpy as jnp
from jax import lax
from jax.experimental import pallas as pl
from jax.experimental.pallas import tpu as pltpu
from jax.sharding import PartitionSpec as P

H = 8
HD = 64
LANES = 2 * HD
WIDE = H * LANES
SPAN = 512
NEAR = 4
SCALE = HD ** (-0.5)
NEG = -1e30
SHUT = 100.0
EPS = 1e-06
MIB = 1024 * 1024

F32 = jnp.float32
BF16 = jnp.bfloat16
TOKEN = ((8, LANES), F32)


def dot(left, right):
    return jnp.dot(left, right, preferred_element_type=F32)


def dot_back(left, right):
    return lax.dot_general(left, right, (((1,), (1,)), ((), ())), preferred_element_type=F32)


def rows_dot(left, right):
    return lax.dot_general(left, right, (((0,), (0,)), ((), ())), preferred_element_type=F32)


def cost_of(microseconds):
    return pl.CostEstimate(flops=int(microseconds * 1e9), bytes_accessed=int(microseconds * 3e6), transcendentals=0)


def block_rows(rows):
    return 256 if rows % 256 == 0 else rows


def head_lanes(h):
    return slice(h * LANES, (h + 1) * LANES)


TILE = 256
REACH = SPAN + TILE
HEADS = 2
BACK_HEADS = 1
CHUNKS = 32
EARLY_ROWS = 128
LATE_ROWS = 64
EXTRA_ROWS = 16


def window_parts(first):
    before = max(SPAN - first, 0)
    parts = [(True, SPAN - before, before)] if before else []
    return parts + [(False, max(first - SPAN, 0), REACH - before)]


def window_keys(halo_ref, own_ref, first, lanes):
    return [(halo_ref if halo else own_ref)[at : at + n, lanes] for halo, at, n in window_parts(first)]


def window_bias(query_axis):
    shape = (TILE, REACH) if query_axis == 0 else (REACH, TILE)
    query = lax.broadcasted_iota(jnp.int32, shape, query_axis)
    key = lax.broadcasted_iota(jnp.int32, shape, 1 - query_axis)
    return jnp.where((key > query) & (key <= query + SPAN), 0.0, NEG)


def masked(scores, bias, first, base, key_axis):
    cut = lambda v, i, j: v[i:j] if key_axis == 0 else v[:, i:j]
    out = []
    for at in range(0, REACH, TILE):
        part = cut(scores, at, at + TILE)
        if at == 0 or at == SPAN:
            part = part + cut(bias, at, at + TILE)
        if first + at < SPAN:
            part = part + jnp.where(base + first + at >= SPAN, 0.0, NEG)
        out.append(part)
    return jnp.concatenate(out, axis=key_axis)


def pipelined(work, before, middle, after):
    ready = before(*work[0])
    held = None
    for k, item in enumerate(work):
        following = before(*work[k + 1]) if k + 1 < len(work) else None
        done = middle(item, ready)
        if held is not None:
            after(*held)
        held, ready = (item, done), following
    after(*held)


def local_kernel(start, base_ref, ask_ref, halo_ref, own_ref, out_ref, total_ref, bias_ref, totals):
    step = pl.program_id(0)
    base = base_ref[0]

    @pl.when(step == 0)
    def fill():
        bias_ref[...] = window_bias(0)

    lane = lax.broadcasted_iota(jnp.int32, (TILE, LANES), 1)

    def scores(at, g):
        query = jnp.where(lane < HD, ask_ref[at : at + TILE, head_lanes(g)], 0.0).astype(BF16)
        return jnp.concatenate([dot_back(query, k) for k in window_keys(halo_ref, own_ref, start + at, head_lanes(g))], axis=1)

    def softmax(item, raw):
        raw = masked(raw, bias_ref, start + item[0], base, 1)
        top = jnp.max(raw, axis=1, keepdims=True)
        expo = jnp.exp(raw - top)
        return expo.astype(BF16), jnp.sum(expo, axis=1, keepdims=True), top

    def finish(item, done):
        at, g = item
        expo, total, top = done
        out, column = None, 0
        for keys in window_keys(halo_ref, own_ref, start + at, head_lanes(g)):
            term = dot(expo[:, column : column + keys.shape[0]], keys)
            column += keys.shape[0]
            out = term if out is None else out + term
        here = slice(at, at + TILE)
        out_ref[here, head_lanes(g)] = (out * (1.0 / total)).astype(BF16)
        totals[here, :] = jnp.where(lane == step * HEADS + g, top + jnp.log(total), totals[here, :])

    pipelined([(at, g) for g in range(HEADS) for at in range(0, ask_ref.shape[0], TILE)], scores, softmax, finish)

    @pl.when(step == H // HEADS - 1)
    def turn():
        for at in range(0, ask_ref.shape[0], LANES):
            total_ref[:, at : at + LANES] = totals[at : at + LANES, :].T[:H, :]


def local_attention(base, ask, halo, own, start, stop, earlier=(), after=()):
    rows = ask.shape[0]
    count = stop - start
    wide = HEADS * LANES
    part = lambda h: (start // count, h)
    held = [pl.BlockSpec(memory_space=pl.ANY)] * (len(earlier) + len(after))
    return pl.pallas_call(
        lambda *refs: local_kernel(start, *refs[:4], *refs[4 + len(held) :]),
        grid=(H // HEADS,),
        in_specs=[
            pl.BlockSpec(memory_space=pltpu.SMEM),
            pl.BlockSpec((count, wide), part),
            pl.BlockSpec((SPAN, wide), lambda h: (0, h)),
            pl.BlockSpec((rows, wide), lambda h: (0, h)),
        ]
        + held,
        out_specs=[pl.BlockSpec((count, wide), part), pl.BlockSpec((H, count), lambda h: (0, start // count))],
        out_shape=[pltpu.HBM((rows, WIDE), BF16), pltpu.HBM((H, rows), F32)],
        scratch_shapes=[pltpu.VMEM((TILE, REACH), F32), pltpu.VMEM((count, LANES), F32)],
        input_output_aliases={4 + k: k for k in range(len(earlier))},
        compiler_params=pltpu.CompilerParams(vmem_limit_bytes=12 * MIB),
        cost_estimate=cost_of(count / 80),
        name="local_attention",
    )(base, *in_hbm(ask, halo, own, *earlier), *after)


def local_back_kernel(
    first_step, base_ref, ask_ref, halo_ref, own_ref, grad_ref, total_ref, inner_ref, partial_ref, far_grad_ref,
    ask_grad_ref, memory_grad_ref, sums_ref, bias_ref,
):
    step = pl.program_id(0) + first_step
    rows = ask_ref.shape[0]
    base = base_ref[0]
    start = far_grad_ref.shape[0] - rows - SPAN

    @pl.when(step == first_step)
    def fill():
        bias_ref[...] = window_bias(1)

    left = left_lanes(TILE)
    sums_ref[...] = far_grad_ref[...].astype(F32)

    def query_of(first, g):
        return jnp.where(left, ask_ref[first : first + TILE, head_lanes(g)], 0.0).astype(BF16)

    def products(first, g):
        keys = window_keys(halo_ref, own_ref, first, head_lanes(g))
        query, grad = query_of(first, g), grad_ref[first : first + TILE, head_lanes(g)]
        join = lambda rows: jnp.concatenate([dot_back(k, rows) for k in keys], axis=0)
        return join(query), join(grad)

    def score_grads(item, done):
        first, g = item
        scores, prob_grad = done
        here = slice(first, first + TILE)
        total = total_ref[pl.ds(step * BACK_HEADS + g, 1), here]
        inner = inner_ref[pl.ds(step * BACK_HEADS + g, 1), here]
        probs = jnp.exp(masked(scores, bias_ref, first, base, 0) - total)
        return (probs * (prob_grad - inner)).astype(BF16), probs.astype(BF16)

    def finish(item, done):
        first, g = item
        score_grad, probs = done
        here, lanes = slice(first, first + TILE), head_lanes(g)
        query_grad, row = None, 0
        for keys in window_keys(halo_ref, own_ref, first, lanes):
            term = rows_dot(score_grad[row : row + keys.shape[0]], keys)
            row += keys.shape[0]
            query_grad = term if query_grad is None else query_grad + term
        sums_ref[start + first : start + first + REACH, lanes] += dot(score_grad, query_of(first, g)) + dot(
            probs, grad_ref[here, lanes]
        )
        partial = partial_ref[here, lanes].astype(F32)
        ask_grad_ref[here, lanes] = (partial + jnp.where(left, query_grad * SCALE, 0.0)).astype(BF16)

    pipelined([(first, g) for g in range(BACK_HEADS) for first in range(0, rows, TILE)], products, score_grads, finish)
    memory_grad_ref[...] = sums_ref[...].astype(BF16)


def local_attention_back(base, ask, halo, own, grad, total, inner, partial, far_grad, steps, earlier=(), after=()):
    rows = ask.shape[0]
    length = far_grad.shape[0]
    first = steps[0]
    head = lambda n: pl.BlockSpec((n, BACK_HEADS * LANES), lambda h: (0, h + first))
    flat = pl.BlockSpec((H, rows), lambda h: (0, 0))
    held = [pl.BlockSpec(memory_space=pl.ANY)] * (len(earlier) + len(after))
    return pl.pallas_call(
        lambda *refs: local_back_kernel(first, *refs[:9], *refs[9 + len(held) :]),
        grid=(len(steps),),
        in_specs=[
            pl.BlockSpec(memory_space=pltpu.SMEM),
            head(rows),
            pl.BlockSpec((SPAN, BACK_HEADS * LANES), lambda h: (0, h + first)),
            head(rows),
            head(rows),
            flat,
            flat,
            head(rows),
            head(length),
        ]
        + held,
        out_specs=[head(rows), head(length)],
        out_shape=[
            pltpu.HBM((rows, WIDE), BF16),
            pltpu.HBM((length, WIDE), BF16),
        ],
        scratch_shapes=[pltpu.VMEM((length, BACK_HEADS * LANES), F32), pltpu.VMEM((REACH, TILE), F32)],
        input_output_aliases={9 + k: k for k in range(len(earlier))},
        compiler_params=pltpu.CompilerParams(vmem_limit_bytes=20 * MIB),
        cost_estimate=cost_of(0.3),
        name="local_attention_back",
    )(base, *in_hbm(ask, halo, own, grad, total, inner, partial, far_grad, *earlier), *after)


def token_tile(ref, token):
    return ref[pl.ds(pl.multiple_of(token * H, H), H), :]


def put_heads(ref, h, values):
    ref[pl.ds(h, values.shape[0], stride=H), :] = values


def take_heads(ref, h, count):
    return ref[pl.ds(h, count, stride=H), :]


def left_lanes(count):
    return lax.broadcasted_iota(jnp.int32, (count, LANES), 1) < HD


def build_table(table, *refs):
    block, base = 128, 0
    for ref in refs:

        def rows(k, carry, ref=ref, base=base):
            here = pl.ds(pl.multiple_of(k * block, block), block)
            for h in range(H):
                there = pl.ds(pl.multiple_of((base + k * block) * H, block * H) + h, block, stride=H)
                table[there, :] = ref[here, head_lanes(h)].astype(F32)
            return carry

        lax.fori_loop(0, ref.shape[0] // block, rows, 0)
        base += ref.shape[0]


def row_sums(values):
    return jnp.sum(values, axis=1, keepdims=True)


def softmax_over(match):
    top = functools.reduce(jnp.maximum, match)
    expo = [jnp.exp(m - top) for m in match]
    scale = 1.0 / functools.reduce(jnp.add, expo)
    return [e * scale for e in expo]


TOKENS = 128
GROUP = 4


def lane_sums(values):
    return dot(values.astype(BF16), jnp.ones((LANES, LANES), BF16))


def gather_group(index_ref, table, near_rows, first, group):
    for k in range(GROUP):
        t = group * GROUP + k
        for j in range(NEAR):
            near_rows[j, t * H : (t + 1) * H, :] = token_tile(table, index_ref[(first + t) * NEAR + j])


def scatter_group(index_ref, sums, terms, first, group):
    for k in range(GROUP):
        t = group * GROUP + k
        for j in range(NEAR):
            there = pl.ds(pl.multiple_of(index_ref[(first + t) * NEAR + j] * H, H), H)
            held = sums[j % len(sums)]
            held[there, :] = held[there, :] + terms[j, t * H : (t + 1) * H, :]


def retrieve_kernel(
    index_ref, far_ref, halo_ref, own_ref, ask_ref, local_ref, near_ref, weight_ref, blended_ref,
    table, ask_rows, out_rows, near_rows,
):
    step = pl.program_id(0)
    count = ask_ref.shape[0]
    first = step * count

    @pl.when(step == 0)
    def build():
        build_table(table, far_ref, halo_ref, own_ref)

    for h in range(H):
        put_heads(ask_rows, h, ask_ref[:, head_lanes(h)].astype(F32))
    left = left_lanes(GROUP * H)
    groups = count // GROUP
    rows_of = lambda group: slice(group * GROUP * H, (group + 1) * GROUP * H)

    def match(group):
        if group + 1 < groups:
            gather_group(index_ref, table, near_rows, first, group + 1)
        here = rows_of(group)
        query = jnp.where(left, ask_rows[here, :], 0.0)
        return [(lane_sums if j > 1 else row_sums)(near_rows[j, here, :] * query) for j in range(NEAR)]

    def weights(item, done):
        return softmax_over(done)

    def recall(item, weight):
        here = rows_of(item[0])
        out_rows[here, :] = functools.reduce(jnp.add, [weight[j] * near_rows[j, here, :] for j in range(NEAR)])
        for j in range(NEAR):
            weight_ref[j, here, :] = weight[j].astype(BF16)
            near_ref[j, here, :] = near_rows[j, here, :].astype(BF16)

    gather_group(index_ref, table, near_rows, first, 0)
    pipelined([(group,) for group in range(groups)], match, weights, recall)
    left = left_lanes(count)
    for h in range(H):
        lanes = head_lanes(h)
        local = local_ref[:, lanes].astype(F32)
        mix = 1.0 - jax.nn.sigmoid(ask_ref[:, lanes].astype(F32))
        blended = local + mix * (take_heads(out_rows, h, count) - local)
        blended_ref[:, lanes] = jnp.where(left, 0.0, blended).astype(BF16)


def retrieve(index, far, halo, own, ask, local):
    rows = ask.shape[0]
    length = far.shape[0] + halo.shape[0] + rows
    count = min(TOKENS, rows)
    wide = pl.BlockSpec((count, WIDE), lambda c: (c, 0))
    tall = pl.BlockSpec((NEAR, count * H, LANES), lambda c: (0, c, 0))
    return pl.pallas_call(
        retrieve_kernel,
        grid=(rows // count,),
        in_specs=[
            pl.BlockSpec(memory_space=pltpu.SMEM),
            pl.BlockSpec(far.shape, lambda c: (0, 0)),
            pl.BlockSpec(halo.shape, lambda c: (0, 0)),
            pl.BlockSpec(own.shape, lambda c: (0, 0)),
            wide,
            wide,
        ],
        out_specs=[tall, tall, wide],
        out_shape=[
            pltpu.HBM((NEAR, rows * H, LANES), BF16),
            pltpu.HBM((NEAR, rows * H, LANES), BF16),
            jax.ShapeDtypeStruct((rows, WIDE), BF16),
        ],
        scratch_shapes=[
            pltpu.VMEM((length * H, LANES), F32),
            pltpu.VMEM((count * H, LANES), F32),
            pltpu.VMEM((count * H, LANES), F32),
            pltpu.VMEM((NEAR, count * H, LANES), F32),
        ],
        compiler_params=pltpu.CompilerParams(vmem_limit_bytes=28 * MIB),
        cost_estimate=cost_of(12),
        name="retrieve",
    )(index, *in_hbm(far, halo, own, ask, local))


def retrieve_back_kernel(
    index_ref, grad_ref, ask_ref, local_ref, near_ref, weight_ref,
    local_grad_ref, inner_ref, partial_ref, far_ref,
    sums_even, sums_odd, ask_rows, grad_rows, out_rows, mixed, terms,
):
    step = pl.program_id(0)
    count = ask_ref.shape[0]
    first = step * count
    length = far_ref.shape[0]

    @pl.when(step == 0)
    def clear():
        block = 1024

        def rows(k, carry):
            here = pl.ds(pl.multiple_of(k * block, block), block)
            sums_even[here, :] = jnp.zeros((block, LANES), F32)
            sums_odd[here, :] = jnp.zeros((block, LANES), F32)
            return carry

        lax.fori_loop(0, length * H // block, rows, 0)

    left = left_lanes(count)
    lane = lax.broadcasted_iota(jnp.int32, (count, LANES), 1)
    inner_all = jnp.zeros((count, LANES), F32)
    for h in range(H):
        lanes = head_lanes(h)
        grad = grad_ref[:, lanes].astype(F32)
        ask = ask_ref[:, lanes].astype(F32)
        mix = 1.0 - jax.nn.sigmoid(ask)
        inner = row_sums(grad * local_ref[:, lanes].astype(F32))
        inner_all = jnp.where(lane == HD + h, inner - mix * inner, inner_all)
        mixed[:, lanes] = mix * inner
        local_grad_ref[:, lanes] = (grad - mix * grad).astype(BF16)
        put_heads(ask_rows, h, jnp.where(left, ask, mix))
        put_heads(grad_rows, h, grad)
    inner_ref[...] = inner_all.T[HD : HD + H, :]
    groups = count // GROUP
    left_tile = left_lanes(GROUP * H)
    sums = (sums_even, sums_odd)
    rows_of = lambda group: slice(group * GROUP * H, (group + 1) * GROUP * H)

    def weight_grads(group):
        here = rows_of(group)
        grad = ask_rows[here, :] * grad_rows[here, :]
        return [(lane_sums if j > 1 else row_sums)(near_ref[j, here, :].astype(F32) * grad) for j in range(NEAR)]

    def match_grads(item, weight_grad):
        here = rows_of(item[0])
        weight = [weight_ref[j, here, :].astype(F32) for j in range(NEAR)]
        inner = functools.reduce(jnp.add, [w * g for w, g in zip(weight, weight_grad)])
        match_grad = [w * (g - inner) for w, g in zip(weight, weight_grad)]
        query_grad = functools.reduce(
            jnp.add, [g * near_ref[j, here, :].astype(F32) for j, g in enumerate(match_grad)]
        )
        out_rows[here, :] = jnp.where(left_tile, query_grad * SCALE, inner)
        ask = ask_rows[here, :]
        source = jnp.where(left_tile, ask, ask * grad_rows[here, :])
        for j in range(NEAR):
            terms[j, here, :] = jnp.where(left_tile, match_grad[j], weight[j]) * source

    def add_terms(item, done):
        scatter_group(index_ref, sums, terms, first, item[0])

    pipelined([(group,) for group in range(groups)], weight_grads, match_grads, add_terms)
    for h in range(H):
        lanes = head_lanes(h)
        tile = take_heads(out_rows, h, count)
        gate = jax.nn.sigmoid(ask_ref[:, lanes].astype(F32))
        partial_ref[:, lanes] = jnp.where(left, tile, (gate / HD) * (mixed[:, lanes] - tile)).astype(BF16)

    @pl.when(step == pl.num_programs(0) - 1)
    def finish():
        block = 128

        def rows(k, carry):
            here = pl.ds(pl.multiple_of(k * block, block), block)
            for h in range(H):
                there = pl.ds(pl.multiple_of(k * (block * H), block * H) + h, block, stride=H)
                far_ref[here, head_lanes(h)] = (sums_even[there, :] + sums_odd[there, :]).astype(BF16)
            return carry

        lax.fori_loop(0, length // block, rows, 0)


def retrieve_back(index, grad, ask, local, near, weight, length, after=()):
    rows = ask.shape[0]
    count = min(TOKENS, rows)
    wide = pl.BlockSpec((count, WIDE), lambda c: (c, 0))
    tall = pl.BlockSpec((NEAR, count * H, LANES), lambda c: (0, c, 0))
    return pl.pallas_call(
        lambda *refs: retrieve_back_kernel(*refs[:6], *refs[6 + len(after) :]),
        grid=(rows // count,),
        in_specs=[
            pl.BlockSpec(memory_space=pltpu.SMEM),
            wide,
            wide,
            wide,
            tall,
            tall,
        ]
        + [pl.BlockSpec(memory_space=pl.ANY)] * len(after),
        out_specs=[
            wide,
            pl.BlockSpec((H, count), lambda c: (0, c)),
            wide,
            pl.BlockSpec((length, WIDE), lambda c: (0, 0)),
        ],
        out_shape=[
            pltpu.HBM((rows, WIDE), BF16),
            pltpu.HBM((H, rows), F32),
            pltpu.HBM((rows, WIDE), BF16),
            pltpu.HBM((length, WIDE), BF16),
        ],
        scratch_shapes=[
            pltpu.VMEM((length * H, LANES), F32),
            pltpu.VMEM((length * H, LANES), F32),
            pltpu.VMEM((count * H, LANES), F32),
            pltpu.VMEM((count * H, LANES), F32),
            pltpu.VMEM((count * H, LANES), F32),
            pltpu.VMEM((count, WIDE), F32),
            pltpu.VMEM((NEAR, count * H, LANES), F32),
        ],
        compiler_params=pltpu.CompilerParams(vmem_limit_bytes=40 * MIB),
        cost_estimate=cost_of(24),
        name="retrieve_back",
    )(index, *in_vmem(grad), *in_hbm(ask, local, near, weight), *after)


def turned(block, shift):
    size = lax.axis_size("seq")
    return lax.ppermute(block, "seq", [((i + shift) % size, i) for i in range(size)])


def index_bits(axis):
    return [(axis, b) for b in range(lax.axis_size(axis).bit_length() - 1)]


def level_groups():
    dp, seq = index_bits("dp"), index_bits("seq")
    return [dp[:1], dp[1:3], seq[:1] + dp[3:4]], dp[4:] + seq[1:]


def own_place(group):
    place = 0
    for k, (axis, bit) in enumerate(group):
        place = place + (((lax.axis_index(axis) >> bit) & 1) << k)
    return place


def own_chunk():
    chunk = 0
    for group in level_groups()[0]:
        chunk = (chunk << len(group)) + own_place(group)
    return jnp.reshape(chunk, (1,)).astype(jnp.int32)


def swapped(block, group, distance):
    flips = {"dp": 0, "seq": 0}
    for k, (axis, bit) in enumerate(group):
        if (distance >> k) & 1:
            flips[axis] |= 1 << bit
    n_dp, n_seq = lax.axis_size("dp"), lax.axis_size("seq")
    if not flips["seq"]:
        return lax.ppermute(block, "dp", [(i, i ^ flips["dp"]) for i in range(n_dp)])
    if not flips["dp"]:
        return lax.ppermute(block, "seq", [(i, i ^ flips["seq"]) for i in range(n_seq)])
    route = [(i, (i // n_seq ^ flips["dp"]) * n_seq + (i % n_seq ^ flips["seq"])) for i in range(n_dp * n_seq)]
    return lax.ppermute(block, ("dp", "seq"), route)


def in_hbm(*arrays):
    return [pltpu.with_memory_space_constraint(v, pltpu.HBM) for v in arrays]


def in_vmem(*arrays):
    return [pltpu.with_memory_space_constraint(v, pltpu.VMEM) for v in arrays]


def whole_call(kernel, name, *operands, outs, scratch=(), after=(), cost=0.3, spare=4, resident=(), streamed=(), inside=(), after_far=()):
    count, late = len(operands), len(streamed)
    operands = [in_hbm(v)[0] if k in streamed else v for k, v in enumerate(operands)]
    operands = [in_vmem(v)[0] if k in inside else v for k, v in enumerate(operands)]

    def place(k, v):
        if v.dtype == jnp.int32:
            return pltpu.SMEM
        return pltpu.HBM if k in streamed else pltpu.VMEM

    held = [pltpu.VMEM(operands[k].shape, operands[k].dtype) for k in streamed]
    shapes = [(v.shape, v.dtype) for k, v in enumerate(operands) if k not in inside]
    shapes += [(v.shape, v.dtype) for v in scratch]
    shapes += [out for k, out in enumerate(outs) if k not in resident]
    size = sum(math.prod(shape) * jnp.dtype(dtype).itemsize for shape, dtype in shapes)

    def wrapped(*refs):
        ins, rest = list(refs[:count]), refs[count + len(after) + len(after_far) :]
        if not late:
            return kernel(*ins, *rest)
        rest, copies = rest[: -2 * late], {}
        for n, k in enumerate(streamed):
            held_ref, sem = refs[-2 * late + n], refs[-late + n]
            copies[k] = pltpu.make_async_copy(ins[k], held_ref, sem)
            copies[k].start()
            ins[k] = held_ref
        return kernel(lambda k: copies[k].wait(), *ins, *rest)

    return pl.pallas_call(
        wrapped,
        in_specs=[pl.BlockSpec(memory_space=place(k, v)) for k, v in enumerate(operands)]
        + [pl.BlockSpec(memory_space=pl.ANY)] * len(after)
        + [pl.BlockSpec(memory_space=pltpu.HBM)] * len(after_far),
        out_specs=[pl.BlockSpec(memory_space=pltpu.VMEM)] * len(outs),
        out_shape=[
            pltpu.VMEM(shape, dtype) if k in resident else jax.ShapeDtypeStruct(shape, dtype)
            for k, (shape, dtype) in enumerate(outs)
        ],
        scratch_shapes=list(scratch) + held + [pltpu.SemaphoreType.DMA(())] * late,
        compiler_params=pltpu.CompilerParams(vmem_limit_bytes=size + spare * MIB),
        cost_estimate=cost_of(cost),
        name=name,
    )(*operands, *after, *in_hbm(*after_far))


def add_pieces(own, arrived, pieces, extra=0, **order):
    rows, width = own.shape
    count = (rows - extra) // pieces

    def kernel(*refs):
        terms, outs = refs[: 1 + len(arrived)], refs[1 + len(arrived) :]

        def total(here):
            values = terms[0][here, :].astype(F32)
            for term in terms[1:]:
                values = values + term[here, :].astype(F32)
            return values.astype(BF16)

        for k, out in enumerate(outs):
            out[:count, :] = total(slice(k * count, (k + 1) * count))
        if extra:
            last = total(slice(rows - extra, rows))
            for out in outs:
                out[count:, :] = last

    outs = [((count + extra, width), BF16)] * pieces
    return whole_call(kernel, "add_pieces", own, *arrived, outs=outs, **order)


def join_pieces(pieces, **order):
    count, width = pieces[0].shape

    def kernel(*refs):
        for k, ref in enumerate(refs[:-1]):
            refs[-1][k * count : (k + 1) * count, :] = ref[...]

    return whole_call(kernel, "join_pieces", *pieces, outs=[((count * len(pieces), width), BF16)], **order)[0]


def scatter_start(own, send):
    return own, [swapped(send, level_groups()[0][0], 1)]


def scatter_level(held, level, extra=0, **order):
    own, arrived = held
    group = level_groups()[0][level]
    pieces = add_pieces(own, arrived, 2 ** len(group), extra, **order)
    return pieces[0], [swapped(piece, group, d) for d, piece in enumerate(pieces) if d]


def scatter_finish(held, **order):
    total = add_pieces(*held, 1, **order)[0]
    for bit in level_groups()[1]:
        total = add_pieces(total, [swapped(total, [bit], 1)], 1)[0]
    return total


def gather_level(total, level):
    group = level_groups()[0][level]
    return [total] + [swapped(total, group, d) for d in range(1, 2 ** len(group))]


def rms_unit(values):
    scale = lax.rsqrt(jnp.mean(values * values, axis=-1, keepdims=True) + EPS)
    return values * scale, scale


def rms_back(unit, scale, grad):
    return scale * (grad - unit * jnp.mean(grad * unit, axis=-1, keepdims=True))


def lay_weights_kernel(wait, query_ref, key_ref, value_ref, gate_ref, output_ref, ask_ref, memory_ref, blend_ref):
    width = query_ref.shape[0]
    gate = gate_ref[...].astype(F32).T
    for k in (0, 1, 2, 4):
        wait(k)
    for h in range(H):
        here = slice(h * HD, (h + 1) * HD)
        column = jnp.broadcast_to(gate[:, h : h + 1], (width, HD)).astype(BF16)
        ask_ref[:, head_lanes(h)] = jnp.concatenate([query_ref[:, here], column], axis=1)
        memory_ref[:, head_lanes(h)] = jnp.concatenate([key_ref[:, here], value_ref[:, here]], axis=1)
        blend_ref[h * LANES : h * LANES + HD, :] = jnp.zeros((HD, width), BF16)
        blend_ref[h * LANES + HD : (h + 1) * LANES, :] = output_ref[here, :]


def lay_weights(query_weight, key_weight, value_weight, gate_weight, output_weight):
    width = query_weight.shape[0]
    wide = ((width, WIDE), BF16)
    return whole_call(
        lay_weights_kernel,
        "lay_weights",
        query_weight,
        key_weight,
        value_weight,
        gate_weight.T,
        output_weight,
        outs=[wide, wide, ((WIDE, width), BF16)],
        streamed=(0, 1, 2, 4),
    )


def project_kernel(inputs_ref, gain_ref, empty_ref, ask_weight_ref, memory_weight_ref, normed_ref, ask_ref, memory_ref):
    normed = (rms_unit(inputs_ref[...].astype(F32))[0] * gain_ref[0:1, :]).astype(BF16)
    normed_ref[...] = normed
    memory_ref[...] = dot(normed, memory_weight_ref[...]).astype(BF16)
    if ask_ref is not None:
        left = (lax.broadcasted_iota(jnp.int32, (1, WIDE), 1) % LANES) < HD
        ask = dot(normed, ask_weight_ref[...])
        block = normed.shape[0]
        row = lax.broadcasted_iota(jnp.int32, (block, block), 0)
        column = lax.broadcasted_iota(jnp.int32, (block, block), 1)
        here = pl.ds(pl.multiple_of(pl.program_id(0) * block, block), block)
        empty = jnp.sum(jnp.where(row == column, empty_ref[:, here].astype(F32), 0.0), axis=1, keepdims=True)
        gate = jnp.where(empty > 0.0, SHUT, ask)
        ask_ref[...] = jnp.where(left, ask * SCALE, gate).astype(BF16)


def row_blocks_call(kernel, name, *operands, outs, cost):
    rows = operands[0].shape[0]
    block = block_rows(rows)
    rows_spec = lambda width: pl.BlockSpec((block, width), lambda k: (k, 0))
    whole = lambda v: pl.BlockSpec(v.shape, lambda k: (0, 0))
    return pl.pallas_call(
        kernel,
        grid=(rows // block,),
        in_specs=[rows_spec(operands[0].shape[1])] + [whole(v) for v in operands[1:]],
        out_specs=[rows_spec(width) for width in outs],
        out_shape=[pltpu.HBM((rows, width), BF16) for width in outs],
        compiler_params=pltpu.CompilerParams(vmem_limit_bytes=14 * MIB),
        cost_estimate=cost_of(cost),
        name=name,
    )(*operands)


def project(inputs, gain, empty, ask_weight, memory_weight):
    width = inputs.shape[1]
    return row_blocks_call(
        project_kernel, "project", inputs, gain, empty, ask_weight, memory_weight, outs=[width, WIDE, WIDE], cost=3
    )


def project_memory(inputs, gain, memory_weight):
    def kernel(inputs_ref, gain_ref, weight_ref, normed_ref, memory_ref):
        project_kernel(inputs_ref, gain_ref, None, None, weight_ref, normed_ref, None, memory_ref)

    return row_blocks_call(
        kernel, "project_memory", inputs, gain, memory_weight, outs=[inputs.shape[1], WIDE], cost=2
    )


ROOT = 0.7978845608028654
CUBE = 0.044715


def gelu_and_slope(x):
    square = x * x
    tanh = jnp.tanh(ROOT * (x * (1.0 + CUBE * square)))
    half = 0.5 * (1.0 + tanh)
    slope = half + (0.5 * ROOT) * x * (1.0 - tanh * tanh) * (1.0 + (3.0 * CUBE) * square)
    return x * half, slope


def hidden_kernel(
    wait, chunk_ref, inputs_ref, cotangent_ref, blended_ref, blend_weight_ref, gain_ref, hidden_weight_ref, return_weight_ref,
    resid_ref, active, hidden_grad, own_ref, send_ref,
    normed, return_sums, hidden_sums,
):
    rows, width = inputs_ref.shape
    hidden = hidden_weight_ref.shape[1]
    block = block_rows(rows)
    gain = gain_ref[0:1, :]
    columns = [slice(at, at + width) for at in range(0, hidden, width)]
    wait(1)

    def row_block(k, carry):
        here = pl.ds(pl.multiple_of(k * block, block), block)
        resid = inputs_ref[here, :].astype(F32) + dot(blended_ref[here, :], blend_weight_ref[...])
        resid_ref[here, :] = resid
        normed_here = (rms_unit(resid)[0] * gain).astype(BF16)
        normed[here, :] = normed_here

        @pl.when(k == 0)
        def weights():
            for n in (2, 6, 7):
                wait(n)

        cotangent = cotangent_ref[here, :]

        def products(lanes):
            return dot(normed_here, hidden_weight_ref[:, lanes]), dot_back(cotangent, return_weight_ref[lanes, :])

        def activate(item, done):
            value, slope = gelu_and_slope(done[0])
            return value.astype(BF16), (done[1] * slope).astype(BF16)

        def keep(item, done):
            active[here, item[0]] = done[0]
            hidden_grad[here, item[0]] = done[1]

        pipelined([(lanes,) for lanes in columns], products, activate, keep)
        return carry

    lax.fori_loop(0, rows // block, row_block, 0)

    def column_block(k, carry):
        lanes = pl.ds(pl.multiple_of(k * width, width), width)
        return_sums[lanes, :] = rows_dot(active[:, lanes], cotangent_ref[...]).astype(BF16)
        hidden_sums[:, lanes] = rows_dot(normed[...], hidden_grad[:, lanes]).astype(BF16)
        return carry

    lax.fori_loop(0, hidden // width, column_block, 0)
    tall, flat = hidden // CHUNKS, width // CHUNKS

    def pack(r, carry):
        for half, out in enumerate((own_ref, send_ref)):
            chunk = chunk_ref[0] ^ (r + half * (CHUNKS // 2))
            rows_at = lambda offset, count: pl.ds(pl.multiple_of(r * EARLY_ROWS + offset, flat), count)
            out[rows_at(0, tall), :] = return_sums[pl.ds(pl.multiple_of(chunk * tall, tall), tall), :]
            for c in range(hidden // width):
                out[rows_at(tall + c * flat, flat), :] = hidden_sums[
                    pl.ds(pl.multiple_of(chunk * flat, flat), flat), c * width : (c + 1) * width
                ]
        return carry

    lax.fori_loop(0, CHUNKS // 2, pack, 0)


def hidden_layer(chunk, inputs, cotangent, blended, blend_weight, gain, hidden_weight, return_weight):
    rows, width = inputs.shape
    hidden = hidden_weight.shape[1]
    half = ((CHUNKS // 2 * EARLY_ROWS, width), BF16)
    return whole_call(
        hidden_kernel,
        "hidden_layer",
        chunk,
        inputs,
        cotangent,
        blended,
        blend_weight,
        gain,
        hidden_weight,
        return_weight,
        outs=[((rows, width), F32), ((rows, hidden), BF16), ((rows, hidden), BF16), half, half],
        scratch=[
            pltpu.VMEM((rows, width), BF16),
            pltpu.VMEM((hidden, width), BF16),
            pltpu.VMEM((width, hidden), BF16),
        ],
        cost=20,
        spare=12,
        resident=(0, 1, 2),
        streamed=(1, 6, 2, 7),
    )


def resid_kernel(
    wait, resid_ref, cotangent_ref, blended_ref, active, hidden_grad, blend_weight_ref, gain_ref, hidden_weight_ref, return_weight_ref,
    outputs_ref, resid_grad_ref, blended_grad_ref, gain_grad_ref, blend_sums_ref,
    resid_grad_b,
):
    rows, width = resid_ref.shape
    block = 2 * block_rows(rows) if rows % 512 == 0 else block_rows(rows)
    gain = gain_ref[0:1, :]
    wait(7)

    def row_block(k, gain_grad):
        here = pl.ds(pl.multiple_of(k * block, block), block)
        resid = resid_ref[here, :]
        unit, scale = rms_unit(resid)
        grad = dot_back(hidden_grad[here, :], hidden_weight_ref[...])

        @pl.when(k == 0)
        def weights():
            wait(8)
            wait(1)

        outputs_ref[here, :] = (resid + dot(active[here, :], return_weight_ref[...])).astype(BF16)
        total = cotangent_ref[here, :].astype(F32) + rms_back(unit, scale, grad * gain)
        resid_grad_ref[here, :] = total
        resid_grad_b[here, :] = total.astype(BF16)
        blended_grad_ref[here, :] = dot_back(total.astype(BF16), blend_weight_ref[...]).astype(BF16)
        return gain_grad + jnp.sum(grad * unit, axis=0, keepdims=True)

    gain_grad = lax.fori_loop(0, rows // block, row_block, jnp.zeros((1, width), F32))
    gain_grad_ref[...] = jnp.broadcast_to(gain_grad, gain_grad_ref.shape)
    blend_sums_ref[...] = rows_dot(blended_ref[...], resid_grad_b[...]).astype(BF16)


def resid_layer(resid, cotangent, blended, active, hidden_grad, blend_weight, gain, hidden_weight, return_weight, after=()):
    rows, width = resid.shape
    return whole_call(
        resid_kernel,
        "resid_layer",
        resid,
        cotangent,
        blended,
        active,
        hidden_grad,
        blend_weight,
        gain,
        hidden_weight,
        return_weight,
        outs=[
            ((rows, width), BF16),
            ((rows, width), F32),
            ((rows, WIDE), BF16),
            ((8, width), F32),
            ((WIDE, width), BF16),
        ],
        scratch=[pltpu.VMEM((rows, width), BF16)],
        after=after,
        cost=8,
        spare=6,
        streamed=(7, 8, 1),
        inside=(0, 3, 4),
        resident=(2,),
    )


def unpack_early_kernel(chunk_ref, own_ref, other_ref, return_ref, hidden_ref, token_ref):
    token_ref[...] = jnp.zeros_like(token_ref)
    width = return_ref.shape[1]
    tall, flat = return_ref.shape[0] // CHUNKS, hidden_ref.shape[0] // CHUNKS
    for r in range(CHUNKS):
        chunk = chunk_ref[0] ^ r
        source = own_ref if r < CHUNKS // 2 else other_ref
        at = (r % (CHUNKS // 2)) * EARLY_ROWS
        return_ref[pl.ds(pl.multiple_of(chunk * tall, tall), tall), :] = source[at : at + tall, :].astype(F32)
        at += tall
        there = pl.ds(pl.multiple_of(chunk * flat, flat), flat)
        for c in range(hidden_ref.shape[1] // width):
            hidden_ref[there, c * width : (c + 1) * width] = source[at : at + flat, :].astype(F32)
            at += flat


def unpack_early(chunk, own, other, return_shape, hidden_shape, after=()):
    outs = [(return_shape, F32), (hidden_shape, F32), TOKEN]
    return whole_call(unpack_early_kernel, "unpack_early", chunk, own, other, outs=outs, after=after)


def late_kernel(
    chunk_ref, far_ref, halo_ref, normed_ref, ask_ref, memory_ref, first_ref, second_ref, blend_ref, own_ref, send_ref, ask_sums, memory_sums
):
    width = normed_ref.shape[1]
    flat = width // CHUNKS
    ask_sums[...] = rows_dot(normed_ref[...], ask_ref[...]).astype(BF16)
    total, at = None, 0
    for ref in (far_ref, halo_ref, normed_ref):
        term = rows_dot(ref[...], memory_ref[at : at + ref.shape[0], :])
        total, at = term if total is None else total + term, at + ref.shape[0]
    memory_sums[...] = total.astype(BF16)
    lane = lax.broadcasted_iota(jnp.int32, (width, LANES), 1)
    small = jnp.zeros((width, LANES), F32)
    for h in range(H):
        at = h * LANES + HD
        small = jnp.where(lane == h, HD * ask_sums[:, at : at + 1].astype(F32), small)
    zeros = jnp.zeros((EXTRA_ROWS - H - 2, width), F32)
    extra = jnp.concatenate([small.T[:H, :], first_ref[0:1, :], second_ref[0:1, :], zeros], axis=0).astype(BF16)
    for out in (own_ref, send_ref):
        out[CHUNKS // 2 * LATE_ROWS :, :] = extra
    for r in range(CHUNKS):
        chunk = chunk_ref[0] ^ r
        out = own_ref if r < CHUNKS // 2 else send_ref
        at = (r % (CHUNKS // 2)) * LATE_ROWS
        here = pl.ds(pl.multiple_of(chunk * flat, flat), flat)
        for pair in range(H // 2):
            lanes = slice(pair * LANES, (pair + 1) * LANES)
            even = slice(2 * pair * LANES, 2 * pair * LANES + HD)
            odd = slice((2 * pair + 1) * LANES, (2 * pair + 1) * LANES + HD)
            out[at : at + flat, lanes] = jnp.concatenate([ask_sums[here, even], ask_sums[here, odd]], axis=1)
        out[at + flat : at + 2 * flat, :] = memory_sums[here, :width]
        out[at + 2 * flat : at + 3 * flat, :] = memory_sums[here, width:]
        row = (chunk // (HD // flat)) * LANES + HD + (chunk % (HD // flat)) * flat
        out[at + 3 * flat : at + 4 * flat, :] = blend_ref[pl.ds(pl.multiple_of(row, flat), flat), :]


def unpack_late_kernel(
    chunk_ref, own_ref, other_ref, extra_ref, query_ref, key_ref, value_ref, output_ref, gate_ref, first_ref, second_ref
):
    width = query_ref.shape[1]
    flat = width // CHUNKS
    for r in range(CHUNKS):
        chunk = chunk_ref[0] ^ r
        source = own_ref if r < CHUNKS // 2 else other_ref
        at = (r % (CHUNKS // 2)) * LATE_ROWS
        there = pl.ds(pl.multiple_of(chunk * flat, flat), flat)
        query_ref[there, :] = source[at : at + flat, :].astype(F32)
        for half in range(2):
            at += flat
            for pair in range(H // 4):
                lanes = slice((half * H // 4 + pair) * LANES, (half * H // 4 + pair + 1) * LANES)
                even = source[at : at + flat, 2 * pair * LANES : (2 * pair + 1) * LANES]
                odd = source[at : at + flat, (2 * pair + 1) * LANES : (2 * pair + 2) * LANES]
                key_ref[there, lanes] = jnp.concatenate([even[:, :HD], odd[:, :HD]], axis=1).astype(F32)
                value_ref[there, lanes] = jnp.concatenate([even[:, HD:], odd[:, HD:]], axis=1).astype(F32)
        at += flat
        output_ref[there, :] = source[at : at + flat, :].astype(F32)
    extra = extra_ref[...].astype(F32)
    gate_ref[...] = extra[:H, :]
    first_ref[...] = extra[H : H + 1, :]
    second_ref[...] = extra[H + 1 : H + 2, :]


def pack_late(chunk, far, halo, normed, ask_grad, memory_grad, first_grad, second_grad, blend_grad, after=()):
    width = normed.shape[1]
    half = ((CHUNKS // 2 * LATE_ROWS + EXTRA_ROWS, width), BF16)
    return whole_call(
        late_kernel,
        "late_weight_grads",
        chunk,
        far,
        halo,
        normed,
        ask_grad,
        memory_grad,
        first_grad,
        second_grad,
        blend_grad,
        outs=[half, half],
        scratch=[pltpu.VMEM((width, WIDE), BF16), pltpu.VMEM((width, WIDE), BF16)],
        after=after,
    )


def unpack_late(chunk, own, other, extra):
    width = own.shape[1]
    square, row = ((width, width), F32), ((1, width), F32)
    return whole_call(
        unpack_late_kernel,
        "unpack_late",
        chunk,
        own,
        other,
        extra,
        outs=[square] * 4 + [((H, width), F32), row, row],
    )


def normed_back_kernel(
    wait, inputs_ref, far_ref, halo_ref, ask_ref, memory_ref, ask_weight_ref, memory_weight_ref, own_grad_ref, others_grad_ref, gain_ref
):
    rows, width = inputs_ref.shape
    length = memory_ref.shape[0]
    block = block_rows(rows)

    def unit(ref, here):
        values = ref[here, :].astype(F32)
        return values * lax.rsqrt(jnp.mean(values * values, axis=-1, keepdims=True) + EPS)

    gain = jnp.zeros((1, width), F32)
    wait(4)
    for at in range(0, length - rows, block):
        here = slice(at, at + block)
        grad = dot_back(memory_ref[here, :], memory_weight_ref[...])
        others_grad_ref[here, :] = grad.astype(BF16)
        past = far_ref.shape[0]
        values = unit(far_ref, here) if at < past else unit(halo_ref, slice(at - past, at - past + block))
        gain = gain + jnp.sum(grad * values, axis=0, keepdims=True)
    wait(3)
    for at in range(0, rows, block):
        here = slice(at, at + block)
        there = slice(length - rows + at, length - rows + at + block)
        grad = dot_back(ask_ref[here, :], ask_weight_ref[...]) + dot_back(memory_ref[there, :], memory_weight_ref[...])
        own_grad_ref[here, :] = grad
        gain = gain + jnp.sum(grad * unit(inputs_ref, here), axis=0, keepdims=True)
    gain_ref[...] = jnp.broadcast_to(gain, gain_ref.shape)


def normed_back(inputs, far, halo, ask_grad, memory_grad, ask_weight, memory_weight, after=()):
    rows, width = inputs.shape
    return whole_call(
        normed_back_kernel,
        "normed_back",
        inputs,
        far,
        halo,
        ask_grad,
        memory_grad,
        ask_weight,
        memory_weight,
        outs=[((rows, width), F32), ((far.shape[0] + halo.shape[0], width), BF16), ((8, width), F32)],
        streamed=(4, 3),
        after=after,
    )


def input_back_kernel(inputs_ref, gain_ref, resid_grad_ref, own_ref, *refs):
    arrived, out_ref, token_ref = refs[:-2], refs[-2], refs[-1]
    token_ref[...] = jnp.zeros_like(token_ref)
    values = inputs_ref[...].astype(F32)
    grad = own_ref[...]
    for ref in arrived:
        grad = grad + ref[...].astype(F32)
    grad = grad * gain_ref[0:1, :]
    scale = lax.rsqrt(jnp.mean(values * values, axis=-1, keepdims=True) + EPS)
    unit = values * scale
    part = scale * (grad - unit * jnp.mean(grad * unit, axis=-1, keepdims=True))
    out_ref[...] = (resid_grad_ref[...] + part).astype(BF16)


def body(
    inputs,
    cotangent,
    neighbours,
    empty_rows,
    first_gain,
    query_weight,
    key_weight,
    value_weight,
    gate_weight,
    output_weight,
    second_gain,
    hidden_weight,
    return_weight,
):
    rows, width = inputs.shape[1:]
    n_seq = lax.axis_size("seq")
    length = rows * n_seq
    base = lax.axis_index("seq") * rows
    base_ref = jnp.reshape(base, (1,)).astype(jnp.int32)
    inputs = inputs.reshape(rows, width)
    cotangent = cotangent.reshape(rows, width)
    if n_seq == 2 and rows > SPAN:
        halo_inputs, far_inputs = turned(inputs[rows - SPAN :], 1), turned(inputs[: rows - SPAN], 1)
    else:
        others = jnp.concatenate([turned(inputs, shift) for shift in range(1, n_seq)], axis=0)
        halo_inputs, far_inputs = others[length - rows - SPAN :], others[: length - rows - SPAN]
    gain_rows = lambda gain: jnp.broadcast_to(gain, (8, width))
    ask_weight, memory_weight, blend_weight = lay_weights(
        query_weight, key_weight, value_weight, gate_weight, output_weight
    )
    chunk = own_chunk()
    index = (neighbours.reshape(rows * NEAR) + (length - rows - base)) % length

    normed, ask, own = project(inputs, gain_rows(first_gain), empty_rows.reshape(1, rows), ask_weight, memory_weight)
    split = SPAN if rows == 2 * SPAN else rows
    attended = ()
    if split < rows:
        attended = local_attention(base_ref, ask, own, own, split, rows)
    halo_normed, halo = project_memory(halo_inputs, gain_rows(first_gain), memory_weight)
    local_out, log_total = local_attention(base_ref, ask, halo, own, 0, split, attended)
    far_normed, far_memory = project_memory(far_inputs, gain_rows(first_gain), memory_weight)
    near, weight, blended = retrieve(index, far_memory, halo, own, ask, local_out)

    resid, active, hidden_grad, early_own, early_send = hidden_layer(
        chunk, inputs, cotangent, blended, blend_weight, gain_rows(second_gain), hidden_weight, return_weight
    )
    early = scatter_start(early_own, early_send)
    outputs, resid_grad, blended_grad, second_gain_grad, blend_grad = resid_layer(
        resid, cotangent, blended, active, hidden_grad, blend_weight, gain_rows(second_gain), hidden_weight, return_weight
    )
    early = scatter_level(early, 1, after=[second_gain_grad])
    local_grad, inner, partial, far = retrieve_back(
        index, blended_grad, ask, local_out, near, weight, length, after=[early[0]]
    )
    early = scatter_level(early, 2, after_far=[inner])
    steps = list(range(H // BACK_HEADS))
    quarter = len(steps) // 4
    back = functools.partial(
        local_attention_back, base_ref, ask, halo, own, local_grad, log_total, inner, partial, far
    )
    grads = back(steps[:quarter], after=[early[0]])
    early_total = scatter_finish(early, after_far=[grads[0]])
    early = gather_level(early_total, 2)
    grads = back(steps[quarter : 2 * quarter], grads, after=[early_total])
    early_total = join_pieces(early, after_far=[grads[0]])
    early = gather_level(early_total, 1)
    ask_grad, memory_grad = back(steps[2 * quarter :], grads, after=[early_total])
    own_grad, others_grad, first_gain_grad = normed_back(
        inputs, far_inputs, halo_inputs, ask_grad, memory_grad, ask_weight, memory_weight
    )
    arrived = [turned(others_grad[(k - 1) * rows : k * rows], n_seq - k) for k in range(1, n_seq)]
    own_late, send_late = pack_late(
        chunk, far_normed, halo_normed, normed, ask_grad, memory_grad, first_gain_grad, second_gain_grad, blend_grad,
        after=[],
    )
    late = scatter_start(own_late, send_late)
    early_own = join_pieces(early, after=[own_late])
    early_other = swapped(early_own, level_groups()[0][0], 1)
    late = scatter_level(late, 1, EXTRA_ROWS, after=[early_own])
    late = scatter_level(late, 2, EXTRA_ROWS)
    input_grad, token = whole_call(
        input_back_kernel, "input_back", inputs, gain_rows(first_gain), resid_grad, own_grad, *arrived,
        outs=[((rows, width), BF16), TOKEN], after=[late[0]],
    )
    late_total = scatter_finish(late, after=[token])
    extra = late_total[LATE_ROWS:]
    late_total = late_total[:LATE_ROWS]
    late = gather_level(late_total, 2)
    return_sum, hidden_sum, token = unpack_early(
        chunk, early_own, early_other, return_weight.shape, hidden_weight.shape, after=[late_total]
    )
    late_total = join_pieces(late, after=[token])
    late = gather_level(late_total, 1)
    late_own = join_pieces(late)
    late_other = swapped(late_own, level_groups()[0][0], 1)
    query_sum, key_sum, value_sum, output_sum, gate_sum, first_sum, second_sum = unpack_late(chunk, late_own, late_other, extra)
    return (
        outputs.reshape(1, rows, width),
        input_grad.reshape(1, rows, width),
        first_sum.reshape(width),
        query_sum,
        key_sum,
        value_sum,
        gate_sum.T,
        output_sum,
        second_sum.reshape(width),
        hidden_sum,
        return_sum,
    )


def solution(mesh):
    split = P("dp", "seq", None)
    in_specs = (split, split, split, P("dp", "seq")) + (P(),) * 9
    out_specs = (split, split) + (P(),) * 9
    return jax.shard_map(body, mesh=mesh, in_specs=in_specs, out_specs=out_specs, check_vma=False)
```

profile of v0, /device:TPU:0, one launch (start us, length us, event | category | flops | bytes accessed | tf_op | source)
XLA Modules:
  0.0 218.2 jit_solution(375297637368448040)
XLA Ops:
  0.7 2.1 slice_bitcast_fusion
  2.7 2.9 %collective-permute-start.1 = (bf16[512,512]{1,0:T(8,128)(2,1)}, bf16[512,512]{1,0:T(8,128)(2,1)S(1)}, u32[]{:S(2)}, u32[]{:S(2)}) collective-permute-start(bf16[512,512]{1,0:T(8,128)(2,1)} %get-tuple-element.151), channel_id=1, source_target_pairs={{1,0},{0,1},{3,2},{2,3},{5,4},{4,5},{7,6},{6,7},{9,8},{8,9},{11,10... | collective-permute-start | bytes 1572872 | tf_op jit(solution)/shard_map/ppermute | solution.py:536
  5.8 0.2 copy.30
  6.0 0.3 add.33
  6.3 2.4 %lay_weights.1 = (bf16[512,1024]{1,0:T(8,128)(2,1)S(1)}, bf16[512,1024]{1,0:T(8,128)(2,1)S(1)}, bf16[1024,512]{1,0:T(8,128)(2,1)S(1)}) custom-call(bf16[512,512]{1,0:T(8,128)(2,1)} %refs_0_.1, bf16[512,512]{1,0:T(8,128)(2,1)} %refs_1_.1, bf16[512,512]{1,0:T(8,128)(2,1)} %refs_2_.1, bf16[8,512]{1,0:T(8,128)(2,1)S(1)} %bitcast.18, bf16[512,512]{1,0:T(8,128)(2,1)} %refs_4_.1), custom_call_target="tpu_custom_call" | custom-call | flops 300000000 | bytes 900000 | tf_op jit(solution)/shard_map/lay_weights/pallas_call | solution.py:612
  8.8 4.4 %project.1 = (bf16[1024,512]{1,0:T(8,128)(2,1)}, bf16[1024,1024]{1,0:T(8,128)(2,1)}, bf16[1024,1024]{1,0:T(8,128)(2,1)}) custom-call(bf16[1024,512]{1,0:T(8,128)(2,1)S(1)} %bitcast.15, f32[8,512]{1,0:T(8,128)S(1)} %broadcast_in_dim.4.gain_ref.refs_1_, s32[1,1024]{1,0:T(1,128)S(1)} %copy-done.8, ...), custom_call_target="tpu_custom_call" | custom-call | flops 3000000000 | bytes 9000000 | tf_op jit(solution)/shard_map/project/pallas_call | solution.py:746
  13.2 7.3 %local_attention.2 = (bf16[1024,1024]{1,0:T(8,128)(2,1)}, f32[8,1024]{1,0:T(8,128)}) custom-call(s32[1]{0:T(128)} %bitcast.6.refs_0_, bf16[1024,1024]{1,0:T(8,128)(2,1)} %get-tuple-element.86.refs_1_.ask_ref.refs_2_, bf16[1024,1024]{1,0:T(8,128)(2,1)} %get-tuple-element.85.refs_2_.refs_3_.own_ref, bf16[1024,1024]{1,0:T(8,128)(2,1)} %get-tuple-element.85.refs_2_.refs_3_.own_ref), custom_call_target="tpu_custom_call" | custom-call | flops 6400000000 | bytes 19200000 | tf_op jit(solution)/shard_map/local_attention/pallas_call | solution.py:150
  20.5 1.9 project_memory.3
  22.4 7.5 %local_attention.3 = (bf16[1024,1024]{1,0:T(8,128)(2,1)}, f32[8,1024]{1,0:T(8,128)}) custom-call(s32[1]{0:T(128)} %bitcast.6.refs_0_, bf16[1024,1024]{1,0:T(8,128)(2,1)} %get-tuple-element.86.refs_1_.ask_ref.refs_2_, bf16[512,1024]{1,0:T(8,128)(2,1)} %get-tuple-element.83.refs_2_.halo_ref, ...), custom_call_target="tpu_custom_call", output_to_operand_aliasing={{0}: (4, {}), {1}: (5, {})} | custom-call | flops 6400000000 | bytes 19200000 | tf_op jit(solution)/shard_map/local_attention/pallas_call | solution.py:150
  29.8 1.9 project_memory.2
  31.7 16.5 %retrieve.1 = (bf16[4,8192,128]{2,1,0:T(8,128)(2,1)}, bf16[4,8192,128]{2,1,0:T(8,128)(2,1)}, bf16[1024,1024]{1,0:T(8,128)(2,1)S(1)}) custom-call(s32[4096]{0:T(1024)S(1)} %add_select_fusion.index_ref.refs_0_, bf16[512,1024]{1,0:T(8,128)(2,1)} %get-tuple-element.82.far_ref, bf16[512,1024]{1,0:T(8,128)(2,1)} %get-tuple-element.83.refs_2_.halo_ref, ...), custom_call_target="tpu_custom_call" | custom-call | flops 12000000000 | bytes 36000000 | tf_op jit(solution)/shard_map/retrieve/pallas_call | solution.py:376
  48.2 17.5 %hidden_layer.1 = (f32[1024,512]{1,0:T(8,128)S(1)}, bf16[1024,2048]{1,0:T(8,128)(2,1)S(1)}, bf16[1024,2048]{1,0:T(8,128)(2,1)S(1)}, bf16[2048,512]{1,0:T(8,128)(2,1)S(1)}, bf16[2048,512]{1,0:T(8,128)(2,1)S(1)}) custom-call(s32[1]{0:T(128)} %bitcast.refs_0_, bf16[1024,512]{1,0:T(8,128)(2,1)} %bitcast.14, bf16[1024,512]{1,0:T(8,128)(2,1)} %bitcast.19, ...), custom_call_target="tpu_custom_call" | custom-call | flops 20000000000 | bytes 60000000 | tf_op jit(solution)/shard_map/hidden_layer/pallas_call | solution.py:612
  65.8 9.7 %resid_layer.1 = (bf16[1024,512]{1,0:T(8,128)(2,1)}, f32[1024,512]{1,0:T(8,128)S(1)}, bf16[1024,1024]{1,0:T(8,128)(2,1)S(1)}, f32[8,512]{1,0:T(8,128)S(1)}, bf16[1024,512]{1,0:T(8,128)(2,1)S(1)}) custom-call(f32[1024,512]{1,0:T(8,128)S(1)} %get-tuple-element.92.refs_0_, bf16[1024,512]{1,0:T(8,128)(2,1)} %bitcast.20, ...), custom_call_target="tpu_custom_call" | custom-call | flops 8000000000 | bytes 24000000 | tf_op jit(solution)/shard_map/resid_layer/pallas_call | solution.py:612
  75.5 0.5 add_pieces.6
  75.9 2.0 collective-permute-start.3
  78.0 1.6 collective-permute-start.4
  79.5 23.1 %retrieve_back.1 = (bf16[1024,1024]{1,0:T(8,128)(2,1)}, f32[8,1024]{1,0:T(8,128)}, bf16[1024,1024]{1,0:T(8,128)(2,1)}, bf16[2048,1024]{1,0:T(8,128)(2,1)}) custom-call(s32[4096]{0:T(1024)S(1)} %add_select_fusion.index_ref.refs_0_, bf16[1024,1024]{1,0:T(8,128)(2,1)S(1)} %get-tuple-element.97.refs_1_, ...), custom_call_target="tpu_custom_call" | custom-call | flops 24000000000 | bytes 72000000 | tf_op jit(solution)/shard_map/retrieve_back/pallas_call | solution.py:495
  102.6 0.4 collective-permute-done.5.refs_3_
  103.0 0.3 add_pieces.7
  103.3 1.7 collective-permute-start.6
  105.0 2.6 %collective-permute-start.7 = (bf16[128,512]{1,0:T(8,128)(2,1)S(1)}, bf16[128,512]{1,0:T(8,128)(2,1)S(1)}, u32[]{:S(2)}, u32[]{:S(2)}) collective-permute-start(bf16[128,512]{1,0:T(8,128)(2,1)S(1)} %get-tuple-element.116), channel_id=1, source_target_pairs={{0,16},{2,18},{4,20},{6,22},{8,24},{10,26},{12,28},{14,30},{16,0},... | collective-permute-start | bytes 393224 | tf_op jit(solution)/shard_map/ppermute | solution.py:569
  107.6 0.2 collective-permute-start.8
  107.7 7.0 %local_attention_back.3 = (bf16[1024,1024]{1,0:T(8,128)(2,1)}, bf16[2048,1024]{1,0:T(8,128)(2,1)}) custom-call(s32[1]{0:T(128)} %bitcast.6.refs_0_, bf16[1024,1024]{1,0:T(8,128)(2,1)} %get-tuple-element.86.refs_1_.ask_ref.refs_2_, bf16[512,1024]{1,0:T(8,128)(2,1)} %get-tuple-element.83.refs_2_.halo_ref, ...), custom_call_target="tpu_custom_call" | custom-call | flops 300000000 | bytes 900000 | tf_op jit(solution)/shard_map/local_attention_back/pallas_call | solution.py:230
  114.7 2.6 %collective-permute-done.7.refs_2_ = bf16[128,512]{1,0:T(8,128)(2,1)S(1)} collective-permute-done((bf16[128,512]{1,0:T(8,128)(2,1)S(1)}, bf16[128,512]{1,0:T(8,128)(2,1)S(1)}, u32[]{:S(2)}, u32[]{:S(2)}) %collective-permute-start.7) | collective-permute-done | bytes 131104 | tf_op jit(solution)/shard_map/ppermute | solution.py:569
  117.3 1.7 collective-permute-done.8.refs_3_
  119.1 3.8 %collective-permute-start.10 = (bf16[128,512]{1,0:T(8,128)(2,1)S(1)}, bf16[128,512]{1,0:T(8,128)(2,1)S(1)}, u32[]{:S(2)}, u32[]{:S(2)}) collective-permute-start(bf16[128,512]{1,0:T(8,128)(2,1)S(1)} %add_pieces.8.refs_11_.refs_0_), channel_id=1, source_target_pairs={{0,16},{2,18},{4,20},{6,22},{8,24},{10,26},{12,28},{14,30},{16,0},... | collective-permute-start | bytes 393224 | tf_op jit(solution)/shard_map/ppermute | solution.py:569
  122.9 0.6 collective-permute-start.9
  123.5 7.0 %local_attention_back.4 = (bf16[1024,1024]{1,0:T(8,128)(2,1)}, bf16[2048,1024]{1,0:T(8,128)(2,1)}) custom-call(s32[1]{0:T(128)} %bitcast.6.refs_0_, bf16[1024,1024]{1,0:T(8,128)(2,1)} %get-tuple-element.86.refs_1_.ask_ref.refs_2_, bf16[512,1024]{1,0:T(8,128)(2,1)} %get-tuple-element.83.refs_2_.halo_ref, ...), custom_call_target="tpu_custom_call", output_to_operand_aliasing={{0}: (9, {}), {1}: (10, {})} | custom-call | flops 300000000 | bytes 900000 | tf_op jit(solution)/shard_map/local_attention_back/pallas_call | solution.py:230
  130.5 1.8 collective-permute-done.11.refs_3_
  132.3 1.3 collective-permute-done.10.refs_2_
  133.8 3.0 %collective-permute-start.15 = (bf16[512,512]{1,0:T(8,128)(2,1)S(1)}, bf16[512,512]{1,0:T(8,128)(2,1)S(1)}, u32[]{:S(2)}, u32[]{:S(2)}) collective-permute-start(bf16[512,512]{1,0:T(8,128)(2,1)S(1)} %join_pieces.4.refs_11_.refs_0_), channel_id=1, source_target_pairs={{0,8},{2,10},{4,12},{6,14},{8,0},{10,2},{12,4},{14,6},{16,24},{18,... | collective-permute-start | bytes 1572872 | tf_op jit(solution)/shard_map/ppermute | solution.py:569
  136.8 0.5 collective-permute-start.14
  137.2 11.7 %local_attention_back.5 = (bf16[1024,1024]{1,0:T(8,128)(2,1)}, bf16[2048,1024]{1,0:T(8,128)(2,1)}) custom-call(s32[1]{0:T(128)} %bitcast.6.refs_0_, bf16[1024,1024]{1,0:T(8,128)(2,1)} %get-tuple-element.86.refs_1_.ask_ref.refs_2_, bf16[512,1024]{1,0:T(8,128)(2,1)} %get-tuple-element.83.refs_2_.halo_ref, ...), custom_call_target="tpu_custom_call", output_to_operand_aliasing={{0}: (9, {}), {1}: (10, {})} | custom-call | flops 300000000 | bytes 900000 | tf_op jit(solution)/shard_map/local_attention_back/pallas_call | solution.py:230
  149.0 6.2 %normed_back.1 = (f32[1024,512]{1,0:T(8,128)S(1)}, bf16[1024,512]{1,0:T(8,128)(2,1)S(1)}, f32[8,512]{1,0:T(8,128)S(1)}) custom-call(bf16[1024,512]{1,0:T(8,128)(2,1)S(1)} %bitcast.16, bf16[512,512]{1,0:T(8,128)(2,1)S(1)} %collective-permute-done.inputs_ref.refs_1_, bf16[512,512]{1,0:T(8,128)(2,1)S(1)} %collective-permute-done.1.inputs_ref.refs_2_, ...), custom_call_target="tpu_custom_call" | custom-call | flops 300000000 | bytes 900000 | tf_op jit(solution)/shard_map/normed_back/pallas_call | solution.py:612
  155.2 3.7 %late_weight_grads.1 = (bf16[1040,512]{1,0:T(8,128)(2,1)S(1)}, bf16[1040,512]{1,0:T(8,128)(2,1)S(1)}) custom-call(s32[1]{0:T(128)} %bitcast.refs_0_, bf16[512,512]{1,0:T(8,128)(2,1)S(1)} %copy-done.6, bf16[512,512]{1,0:T(8,128)(2,1)S(1)} %copy-done.5, bf16[1024,512]{1,0:T(8,128)(2,1)S(1)} %copy-done.4, bf16[1024,1024]{1,0:T(8,128)(2,1)S(1)} %copy-done, ...), custom_call_target="tpu_custom_call" | custom-call | flops 300000000 | bytes 900000 | tf_op jit(solution)/shard_map/late_weight_grads/pallas_call | solution.py:612
  159.0 0.1 join_pieces.5.refs_2_.refs_1_
  159.2 0.5 collective-permute-start.13
  159.7 0.7 collective-permute-start.12
  160.4 4.5 %collective-permute-done.13.refs_1_ = bf16[1040,512]{1,0:T(8,128)(2,1)S(1)} collective-permute-done((bf16[1040,512]{1,0:T(8,128)(2,1)S(1)}, bf16[1040,512]{1,0:T(8,128)(2,1)S(1)}, u32[]{:S(2)}, u32[]{:S(2)}) %collective-permute-start.13) | collective-permute-done | bytes 1064992 | tf_op jit(solution)/shard_map/ppermute | solution.py:569
  164.9 0.2 add_pieces.9
  165.2 1.6 collective-permute-start.17
  166.7 2.0 collective-permute-start.19
  168.7 5.2 %collective-permute-done.17.refs_1_ = bf16[272,512]{1,0:T(8,128)(2,1)S(1)} collective-permute-done((bf16[272,512]{1,0:T(8,128)(2,1)S(1)}, bf16[272,512]{1,0:T(8,128)(2,1)S(1)}, u32[]{:S(2)}, u32[]{:S(2)}) %collective-permute-start.17) | collective-permute-done | bytes 278560 | tf_op jit(solution)/shard_map/ppermute | solution.py:569
  173.9 2.4 %collective-permute-done.18.refs_2_ = bf16[272,512]{1,0:T(8,128)(2,1)S(1)} collective-permute-done((bf16[272,512]{1,0:T(8,128)(2,1)S(1)}, bf16[272,512]{1,0:T(8,128)(2,1)S(1)}, u32[]{:S(2)}, u32[]{:S(2)}) %collective-permute-start.18) | collective-permute-done | bytes 278560 | tf_op jit(solution)/shard_map/ppermute | solution.py:569
  176.3 4.8 %collective-permute-done.19.refs_3_ = bf16[272,512]{1,0:T(8,128)(2,1)S(1)} collective-permute-done((bf16[272,512]{1,0:T(8,128)(2,1)S(1)}, bf16[272,512]{1,0:T(8,128)(2,1)S(1)}, u32[]{:S(2)}, u32[]{:S(2)}) %collective-permute-start.19) | collective-permute-done | bytes 278560 | tf_op jit(solution)/shard_map/ppermute | solution.py:569
  181.1 0.1 add_pieces.10
  181.2 0.7 collective-permute-start.20
  181.9 1.1 collective-permute-start.21
  183.0 2.6 %collective-permute-start.22 = (bf16[80,512]{1,0:T(8,128)(2,1)S(1)}, bf16[80,512]{1,0:T(8,128)(2,1)S(1)}, u32[]{:S(2)}, u32[]{:S(2)}) collective-permute-start(bf16[80,512]{1,0:T(8,128)(2,1)S(1)} %get-tuple-element.139), channel_id=1, source_target_pairs={{0,17},{1,16},{2,19},{3,18},{4,21},{5,20},{6,23},{7,22},{8,25},{9,... | collective-permute-start | bytes 245768 | tf_op jit(solution)/shard_map/ppermute | solution.py:573
  185.7 0.1 collective-permute-done.12.refs_4_
  185.7 2.0 input_back.1
  187.8 2.5 %collective-permute-done.21.refs_2_ = bf16[80,512]{1,0:T(8,128)(2,1)S(1)} collective-permute-done((bf16[80,512]{1,0:T(8,128)(2,1)S(1)}, bf16[80,512]{1,0:T(8,128)(2,1)S(1)}, u32[]{:S(2)}, u32[]{:S(2)}) %collective-permute-start.21) | collective-permute-done | bytes 81952 | tf_op jit(solution)/shard_map/ppermute | solution.py:569
  190.3 1.5 collective-permute-done.22.refs_3_
  191.9 0.2 collective-permute-start.25
  192.1 3.0 %collective-permute-start.24 = (bf16[64,512]{1,0:T(8,128)(2,1)S(1)}, bf16[64,512]{1,0:T(8,128)(2,1)S(1)}, u32[]{:S(2)}, u32[]{:S(2)}) collective-permute-start(bf16[64,512]{1,0:T(8,128)(2,1)S(1)} %slice.24.refs_3_.refs_0_), channel_id=1, source_target_pairs={{0,16},{2,18},{4,20},{6,22},{8,24},{10,26},{12,28},{14,30},{16,0},... | collective-permute-start | bytes 196616 | tf_op jit(solution)/shard_map/ppermute | solution.py:569
  195.1 1.2 collective-permute-start.23
  196.4 3.9 %unpack_early.1 = (f32[2048,512]{1,0:T(8,128)}, f32[512,2048]{1,0:T(8,128)}, f32[8,128]{1,0:T(8,128)S(1)}) custom-call(s32[1]{0:T(128)} %bitcast.refs_0_, bf16[2048,512]{1,0:T(8,128)(2,1)S(1)} %join_pieces.5.refs_2_.refs_1_, bf16[2048,512]{1,0:T(8,128)(2,1)S(1)} %collective-permute-done.26.refs_2_, bf16[64,512]{1,0:T(8,128)(2,1)S(1)} %slice.24.refs_3_.refs_0_), custom_call_target="tpu_custom_call" | custom-call | flops 300000000 | bytes 900000 | tf_op jit(solution)/shard_map/unpack_early/pallas_call | solution.py:612
  200.3 0.8 collective-permute-start.29
  201.1 2.4 %collective-permute-start.28 = (bf16[256,512]{1,0:T(8,128)(2,1)S(1)}, bf16[256,512]{1,0:T(8,128)(2,1)S(1)}, u32[]{:S(2)}, u32[]{:S(2)}) collective-permute-start(bf16[256,512]{1,0:T(8,128)(2,1)S(1)} %join_pieces.6.refs_0_), channel_id=1, source_target_pairs={{0,8},{2,10},{4,12},{6,14},{8,0},{10,2},{12,4},{14,6},{16,24},{18,... | collective-permute-start | bytes 786440 | tf_op jit(solution)/shard_map/ppermute | solution.py:569
  203.5 0.4 collective-permute-start.27
  203.9 6.1 %collective-permute-done.29.refs_3_ = bf16[256,512]{1,0:T(8,128)(2,1)S(1)} collective-permute-done((bf16[256,512]{1,0:T(8,128)(2,1)S(1)}, bf16[256,512]{1,0:T(8,128)(2,1)S(1)}, u32[]{:S(2)}, u32[]{:S(2)}) %collective-permute-start.29) | collective-permute-done | bytes 262176 | tf_op jit(solution)/shard_map/ppermute | solution.py:569
  210.0 3.1 %collective-permute-done.28.refs_2_ = bf16[256,512]{1,0:T(8,128)(2,1)S(1)} collective-permute-done((bf16[256,512]{1,0:T(8,128)(2,1)S(1)}, bf16[256,512]{1,0:T(8,128)(2,1)S(1)}, u32[]{:S(2)}, u32[]{:S(2)}) %collective-permute-start.28) | collective-permute-done | bytes 262176 | tf_op jit(solution)/shard_map/ppermute | solution.py:569
  213.2 2.6 %collective-permute-done.30.refs_2_ = bf16[1024,512]{1,0:T(8,128)(2,1)S(1)} collective-permute-done((bf16[1024,512]{1,0:T(8,128)(2,1)S(1)}, bf16[1024,512]{1,0:T(8,128)(2,1)S(1)}, u32[]{:S(2)}, u32[]{:S(2)}) %collective-permute-start.30) | collective-permute-done | bytes 1048608 | tf_op jit(solution)/shard_map/ppermute | solution.py:569
  215.9 2.4 %unpack_late.1 = (f32[512,512]{1,0:T(8,128)}, f32[512,512]{1,0:T(8,128)}, f32[512,512]{1,0:T(8,128)}, f32[512,512]{1,0:T(8,128)}, f32[8,512]{1,0:T(8,128)}, /*index=5*/f32[1,512]{1,0:T(1,128)}, f32[1,512]{1,0:T(1,128)}) custom-call(s32[1]{0:T(128)} %bitcast.refs_0_, bf16[1024,512]{1,0:T(8,128)(2,1)S(1)} %join_pieces.7.refs_1_, ...), custom_call_target="tpu_custom_call" | custom-call | flops 300000000 | bytes 900000 | tf_op jit(solution)/shard_map/unpack_late/pallas_call | solution.py:612
  (59 shorter events, 0.8 us)
Async XLA Ops:
  0.6 5.1 %copy-start.9 = (s32[1,1024,4]{1,2,0:T(4,128)S(1)}, s32[1,1024,4]{1,2,0:T(4,128)}, u32[]{:S(2)}) copy-start(s32[1,1024,4]{1,2,0:T(4,128)} %param.15) | copy-start | bytes 49156
  0.7 5.6 %copy-start.7 = (bf16[512,8]{0,1:T(8,128)(2,1)S(1)}, bf16[512,8]{0,1:T(8,128)(2,1)}, u32[]{:S(2)}) copy-start(bf16[512,8]{0,1:T(8,128)(2,1)} %param.21) | copy-start | bytes 24580
  2.7 6.0 %copy-start.10 = (f32[512]{0:T(512)S(1)}, f32[512]{0:T(512)}, u32[]{:S(2)}) copy-start(f32[512]{0:T(512)} %param.17) | copy-start | bytes 6148
  2.7 6.0 %copy-start.2 = (bf16[1,1024,512]{2,1,0:T(8,128)(2,1)S(1)}, bf16[1,1024,512]{2,1,0:T(8,128)(2,1)}, u32[]{:S(2)}) copy-start(bf16[1,1024,512]{2,1,0:T(8,128)(2,1)} %param.13) | copy-start | bytes 3145732
  2.7 6.0 %copy-start.8 = (s32[1,1024]{1,0:T(1,128)S(1)}, s32[1,1024]{1,0:T(1,128)}, u32[]{:S(2)}) copy-start(s32[1,1024]{1,0:T(1,128)} %empty_ref.1) | copy-start | bytes 12292
  2.7 17.7 %collective-permute-start.1 = (bf16[512,512]{1,0:T(8,128)(2,1)}, bf16[512,512]{1,0:T(8,128)(2,1)S(1)}, u32[]{:S(2)}, u32[]{:S(2)}) collective-permute-start(bf16[512,512]{1,0:T(8,128)(2,1)} %get-tuple-element.151), channel_id=1, source_target_pairs={{1,0},{0,1},{3,2},{2,3},{5,4},{4,5},{7,6},{6,7},{9,8},{8,9},{11,10... | collective-permute-start | bytes 1572872 | tf_op jit(solution)/shard_map/ppermute | solution.py:536
  5.7 24.1 %collective-permute-start = (bf16[512,512]{1,0:T(8,128)(2,1)S(1)}, bf16[512,512]{1,0:T(8,128)(2,1)S(1)}, u32[]{:S(2)}, u32[]{:S(2)}) collective-permute-start(bf16[512,512]{1,0:T(8,128)(2,1)S(1)} %get-tuple-element.152), channel_id=1, source_target_pairs={{1,0},{0,1},{3,2},{2,3},{5,4},{4,5},{7,6},{6,7},{9,8},{8,9},{11,10... | collective-permute-start | bytes 1572872 | tf_op jit(solution)/shard_map/ppermute | solution.py:536
  31.7 16.5 %copy-start.11 = (f32[512]{0:T(512)S(1)}, f32[512]{0:T(512)}, u32[]{:S(2)}) copy-start(f32[512]{0:T(512)} %param.23) | copy-start | bytes 6148
  65.7 9.8 %collective-permute-start.2 = (bf16[2048,512]{1,0:T(8,128)(2,1)S(1)}, bf16[2048,512]{1,0:T(8,128)(2,1)S(1)}, u32[]{:S(2)}, u32[]{:S(2)}) collective-permute-start(bf16[2048,512]{1,0:T(8,128)(2,1)S(1)} %get-tuple-element.101), channel_id=1, source_target_pairs={{0,2},{2,0},{4,6},{6,4},{8,10},{10,8},{12,14},{14,12},{16,18},{18,... | collective-permute-start | bytes 6291464 | tf_op jit(solution)/shard_map/ppermute | solution.py:569
  75.9 26.7 %collective-permute-start.3 = (bf16[512,512]{1,0:T(8,128)(2,1)S(1)}, bf16[512,512]{1,0:T(8,128)(2,1)S(1)}, u32[]{:S(2)}, u32[]{:S(2)}) collective-permute-start(bf16[512,512]{1,0:T(8,128)(2,1)S(1)} %get-tuple-element.109), channel_id=1, source_target_pairs={{0,4},{2,6},{4,0},{6,2},{8,12},{10,14},{12,8},{14,10},{16,20},{18,... | collective-permute-start | bytes 1572872 | tf_op jit(solution)/shard_map/ppermute | solution.py:569
  78.0 24.6 %collective-permute-start.4 = (bf16[512,512]{1,0:T(8,128)(2,1)S(1)}, bf16[512,512]{1,0:T(8,128)(2,1)S(1)}, u32[]{:S(2)}, u32[]{:S(2)}) collective-permute-start(bf16[512,512]{1,0:T(8,128)(2,1)S(1)} %get-tuple-element.110), channel_id=1, source_target_pairs={{0,8},{2,10},{4,12},{6,14},{8,0},{10,2},{12,4},{14,6},{16,24},{18,... | collective-permute-start | bytes 1572872 | tf_op jit(solution)/shard_map/ppermute | solution.py:569
  79.5 23.5 %collective-permute-start.5 = (bf16[512,512]{1,0:T(8,128)(2,1)S(1)}, bf16[512,512]{1,0:T(8,128)(2,1)S(1)}, u32[]{:S(2)}, u32[]{:S(2)}) collective-permute-start(bf16[512,512]{1,0:T(8,128)(2,1)S(1)} %get-tuple-element.111), channel_id=1, source_target_pairs={{0,12},{2,14},{4,8},{6,10},{8,4},{10,6},{12,0},{14,2},{16,28},{18,... | collective-permute-start | bytes 1572872 | tf_op jit(solution)/shard_map/ppermute | solution.py:569
  103.3 11.4 %collective-permute-start.6 = (bf16[128,512]{1,0:T(8,128)(2,1)S(1)}, bf16[128,512]{1,0:T(8,128)(2,1)S(1)}, u32[]{:S(2)}, u32[]{:S(2)}) collective-permute-start(bf16[128,512]{1,0:T(8,128)(2,1)S(1)} %get-tuple-element.115), channel_id=1, source_target_pairs={{0,1},{1,0},{2,3},{3,2},{4,5},{5,4},{6,7},{7,6},{8,9},{9,8},{10,11... | collective-permute-start | bytes 393224 | tf_op jit(solution)/shard_map/ppermute | solution.py:571
  105.0 12.3 %collective-permute-start.7 = (bf16[128,512]{1,0:T(8,128)(2,1)S(1)}, bf16[128,512]{1,0:T(8,128)(2,1)S(1)}, u32[]{:S(2)}, u32[]{:S(2)}) collective-permute-start(bf16[128,512]{1,0:T(8,128)(2,1)S(1)} %get-tuple-element.116), channel_id=1, source_target_pairs={{0,16},{2,18},{4,20},{6,22},{8,24},{10,26},{12,28},{14,30},{16,0},... | collective-permute-start | bytes 393224 | tf_op jit(solution)/shard_map/ppermute | solution.py:569
  107.6 11.4 %collective-permute-start.8 = (bf16[128,512]{1,0:T(8,128)(2,1)S(1)}, bf16[128,512]{1,0:T(8,128)(2,1)S(1)}, u32[]{:S(2)}, u32[]{:S(2)}) collective-permute-start(bf16[128,512]{1,0:T(8,128)(2,1)S(1)} %get-tuple-element.117), channel_id=1, source_target_pairs={{0,17},{1,16},{2,19},{3,18},{4,21},{5,20},{6,23},{7,22},{8,25},{9,... | collective-permute-start | bytes 393224 | tf_op jit(solution)/shard_map/ppermute | solution.py:573
  119.1 13.3 %collective-permute-start.11 = (bf16[128,512]{1,0:T(8,128)(2,1)S(1)}, bf16[128,512]{1,0:T(8,128)(2,1)S(1)}, u32[]{:S(2)}, u32[]{:S(2)}) collective-permute-start(bf16[128,512]{1,0:T(8,128)(2,1)S(1)} %add_pieces.8.refs_11_.refs_0_), channel_id=1, source_target_pairs={{0,17},{1,16},{2,19},{3,18},{4,21},{5,20},{6,23},{7,22},{8,25},{9,... | collective-permute-start | bytes 393224 | tf_op jit(solution)/shard_map/ppermute | solution.py:573
  119.1 14.5 %collective-permute-start.10 = (bf16[128,512]{1,0:T(8,128)(2,1)S(1)}, bf16[128,512]{1,0:T(8,128)(2,1)S(1)}, u32[]{:S(2)}, u32[]{:S(2)}) collective-permute-start(bf16[128,512]{1,0:T(8,128)(2,1)S(1)} %add_pieces.8.refs_11_.refs_0_), channel_id=1, source_target_pairs={{0,16},{2,18},{4,20},{6,22},{8,24},{10,26},{12,28},{14,30},{16,0},... | collective-permute-start | bytes 393224 | tf_op jit(solution)/shard_map/ppermute | solution.py:569
  122.9 10.7 %collective-permute-start.9 = (bf16[128,512]{1,0:T(8,128)(2,1)S(1)}, bf16[128,512]{1,0:T(8,128)(2,1)S(1)}, u32[]{:S(2)}, u32[]{:S(2)}) collective-permute-start(bf16[128,512]{1,0:T(8,128)(2,1)S(1)} %add_pieces.8.refs_11_.refs_0_), channel_id=1, source_target_pairs={{0,1},{1,0},{2,3},{3,2},{4,5},{5,4},{6,7},{7,6},{8,9},{9,8},{10,11... | collective-permute-start | bytes 393224 | tf_op jit(solution)/shard_map/ppermute | solution.py:571
  133.7 25.3 %collective-permute-start.16 = (bf16[512,512]{1,0:T(8,128)(2,1)S(1)}, bf16[512,512]{1,0:T(8,128)(2,1)S(1)}, u32[]{:S(2)}, u32[]{:S(2)}) collective-permute-start(bf16[512,512]{1,0:T(8,128)(2,1)S(1)} %join_pieces.4.refs_11_.refs_0_), channel_id=1, source_target_pairs={{0,12},{2,14},{4,8},{6,10},{8,4},{10,6},{12,0},{14,2},{16,28},{18,... | collective-permute-start | bytes 1572872 | tf_op jit(solution)/shard_map/ppermute | solution.py:569
  133.8 25.2 %collective-permute-start.15 = (bf16[512,512]{1,0:T(8,128)(2,1)S(1)}, bf16[512,512]{1,0:T(8,128)(2,1)S(1)}, u32[]{:S(2)}, u32[]{:S(2)}) collective-permute-start(bf16[512,512]{1,0:T(8,128)(2,1)S(1)} %join_pieces.4.refs_11_.refs_0_), channel_id=1, source_target_pairs={{0,8},{2,10},{4,12},{6,14},{8,0},{10,2},{12,4},{14,6},{16,24},{18,... | collective-permute-start | bytes 1572872 | tf_op jit(solution)/shard_map/ppermute | solution.py:569
  136.8 22.3 %collective-permute-start.14 = (bf16[512,512]{1,0:T(8,128)(2,1)S(1)}, bf16[512,512]{1,0:T(8,128)(2,1)S(1)}, u32[]{:S(2)}, u32[]{:S(2)}) collective-permute-start(bf16[512,512]{1,0:T(8,128)(2,1)S(1)} %join_pieces.4.refs_11_.refs_0_), channel_id=1, source_target_pairs={{0,4},{2,6},{4,0},{6,2},{8,12},{10,14},{12,8},{14,10},{16,20},{18,... | collective-permute-start | bytes 1572872 | tf_op jit(solution)/shard_map/ppermute | solution.py:569
  137.2 11.7 %copy-start.3 = (bf16[1,1024,512]{2,1,0:T(8,128)(2,1)S(1)}, bf16[1,1024,512]{2,1,0:T(8,128)(2,1)}, u32[]{:S(2)}) copy-start(bf16[1,1024,512]{2,1,0:T(8,128)(2,1)} %param.13) | copy-start | bytes 3145732
  149.0 6.2 %copy-start = (bf16[1024,1024]{1,0:T(8,128)(2,1)S(1)}, bf16[1024,1024]{1,0:T(8,128)(2,1)}, u32[]{:S(2)}) copy-start(bf16[1024,1024]{1,0:T(8,128)(2,1)} %get-tuple-element.120.refs_3_.refs_4_) | copy-start | bytes 6291460
  149.0 6.2 %copy-start.1 = (bf16[2048,1024]{1,0:T(8,128)(2,1)S(1)}, bf16[2048,1024]{1,0:T(8,128)(2,1)}, u32[]{:S(2)}) copy-start(bf16[2048,1024]{1,0:T(8,128)(2,1)} %get-tuple-element.121.refs_4_.refs_5_) | copy-start | bytes 12582916
  149.0 6.2 %copy-start.4 = (bf16[1024,512]{1,0:T(8,128)(2,1)S(1)}, bf16[1024,512]{1,0:T(8,128)(2,1)}, u32[]{:S(2)}) copy-start(bf16[1024,512]{1,0:T(8,128)(2,1)} %get-tuple-element.126.refs_3_) | copy-start | bytes 3145732
  149.0 6.2 %copy-start.5 = (bf16[512,512]{1,0:T(8,128)(2,1)S(1)}, bf16[512,512]{1,0:T(8,128)(2,1)}, u32[]{:S(2)}) copy-start(bf16[512,512]{1,0:T(8,128)(2,1)} %get-tuple-element.125.refs_2_) | copy-start | bytes 1572868
  149.0 6.2 %copy-start.6 = (bf16[512,512]{1,0:T(8,128)(2,1)S(1)}, bf16[512,512]{1,0:T(8,128)(2,1)}, u32[]{:S(2)}) copy-start(bf16[512,512]{1,0:T(8,128)(2,1)} %get-tuple-element.124.refs_1_) | copy-start | bytes 1572868
  159.2 37.2 %collective-permute-start.26 = (bf16[2048,512]{1,0:T(8,128)(2,1)S(1)}, bf16[2048,512]{1,0:T(8,128)(2,1)S(1)}, u32[]{:S(2)}, u32[]{:S(2)}) collective-permute-start(bf16[2048,512]{1,0:T(8,128)(2,1)S(1)} %join_pieces.5.refs_2_.refs_1_), channel_id=1, source_target_pairs={{0,2},{2,0},{4,6},{6,4},{8,10},{10,8},{12,14},{14,12},{16,18},{18,... | collective-permute-start | bytes 6291464 | tf_op jit(solution)/shard_map/ppermute | solution.py:569
  159.2 5.7 %collective-permute-start.13 = (bf16[1040,512]{1,0:T(8,128)(2,1)S(1)}, bf16[1040,512]{1,0:T(8,128)(2,1)S(1)}, u32[]{:S(2)}, u32[]{:S(2)}) collective-permute-start(bf16[1040,512]{1,0:T(8,128)(2,1)S(1)} %get-tuple-element.130), channel_id=1, source_target_pairs={{0,2},{2,0},{4,6},{6,4},{8,10},{10,8},{12,14},{14,12},{16,18},{18,... | collective-permute-start | bytes 3194888 | tf_op jit(solution)/shard_map/ppermute | solution.py:569
  159.7 26.0 %collective-permute-start.12 = (bf16[1024,512]{1,0:T(8,128)(2,1)S(1)}, bf16[1024,512]{1,0:T(8,128)(2,1)S(1)}, u32[]{:S(2)}, u32[]{:S(2)}) collective-permute-start(bf16[1024,512]{1,0:T(8,128)(2,1)S(1)} %get-tuple-element.123), channel_id=1, source_target_pairs={{1,0},{0,1},{3,2},{2,3},{5,4},{4,5},{7,6},{6,7},{9,8},{8,9},{11,10... | collective-permute-start | bytes 3145736 | tf_op jit(solution)/shard_map/ppermute | solution.py:536
  165.2 8.8 %collective-permute-start.17 = (bf16[272,512]{1,0:T(8,128)(2,1)S(1)}, bf16[272,512]{1,0:T(8,128)(2,1)S(1)}, u32[]{:S(2)}, u32[]{:S(2)}) collective-permute-start(bf16[272,512]{1,0:T(8,128)(2,1)S(1)} %get-tuple-element.132), channel_id=1, source_target_pairs={{0,4},{2,6},{4,0},{6,2},{8,12},{10,14},{12,8},{14,10},{16,20},{18,... | collective-permute-start | bytes 835592 | tf_op jit(solution)/shard_map/ppermute | solution.py:569
  166.7 9.5 %collective-permute-start.18 = (bf16[272,512]{1,0:T(8,128)(2,1)S(1)}, bf16[272,512]{1,0:T(8,128)(2,1)S(1)}, u32[]{:S(2)}, u32[]{:S(2)}) collective-permute-start(bf16[272,512]{1,0:T(8,128)(2,1)S(1)} %get-tuple-element.133), channel_id=1, source_target_pairs={{0,8},{2,10},{4,12},{6,14},{8,0},{10,2},{12,4},{14,6},{16,24},{18,... | collective-permute-start | bytes 835592 | tf_op jit(solution)/shard_map/ppermute | solution.py:569
  166.7 14.3 %collective-permute-start.19 = (bf16[272,512]{1,0:T(8,128)(2,1)S(1)}, bf16[272,512]{1,0:T(8,128)(2,1)S(1)}, u32[]{:S(2)}, u32[]{:S(2)}) collective-permute-start(bf16[272,512]{1,0:T(8,128)(2,1)S(1)} %get-tuple-element.134), channel_id=1, source_target_pairs={{0,12},{2,14},{4,8},{6,10},{8,4},{10,6},{12,0},{14,2},{16,28},{18,... | collective-permute-start | bytes 835592 | tf_op jit(solution)/shard_map/ppermute | solution.py:569
  181.2 6.5 %collective-permute-start.20 = (bf16[80,512]{1,0:T(8,128)(2,1)S(1)}, bf16[80,512]{1,0:T(8,128)(2,1)S(1)}, u32[]{:S(2)}, u32[]{:S(2)}) collective-permute-start(bf16[80,512]{1,0:T(8,128)(2,1)S(1)} %get-tuple-element.137), channel_id=1, source_target_pairs={{0,1},{1,0},{2,3},{3,2},{4,5},{5,4},{6,7},{7,6},{8,9},{9,8},{10,11... | collective-permute-start | bytes 245768 | tf_op jit(solution)/shard_map/ppermute | solution.py:571
  181.9 8.3 %collective-permute-start.21 = (bf16[80,512]{1,0:T(8,128)(2,1)S(1)}, bf16[80,512]{1,0:T(8,128)(2,1)S(1)}, u32[]{:S(2)}, u32[]{:S(2)}) collective-permute-start(bf16[80,512]{1,0:T(8,128)(2,1)S(1)} %get-tuple-element.138), channel_id=1, source_target_pairs={{0,16},{2,18},{4,20},{6,22},{8,24},{10,26},{12,28},{14,30},{16,0},... | collective-permute-start | bytes 245768 | tf_op jit(solution)/shard_map/ppermute | solution.py:569
  183.0 8.8 %collective-permute-start.22 = (bf16[80,512]{1,0:T(8,128)(2,1)S(1)}, bf16[80,512]{1,0:T(8,128)(2,1)S(1)}, u32[]{:S(2)}, u32[]{:S(2)}) collective-permute-start(bf16[80,512]{1,0:T(8,128)(2,1)S(1)} %get-tuple-element.139), channel_id=1, source_target_pairs={{0,17},{1,16},{2,19},{3,18},{4,21},{5,20},{6,23},{7,22},{8,25},{9,... | collective-permute-start | bytes 245768 | tf_op jit(solution)/shard_map/ppermute | solution.py:573
  191.9 8.4 %collective-permute-start.25 = (bf16[64,512]{1,0:T(8,128)(2,1)S(1)}, bf16[64,512]{1,0:T(8,128)(2,1)S(1)}, u32[]{:S(2)}, u32[]{:S(2)}) collective-permute-start(bf16[64,512]{1,0:T(8,128)(2,1)S(1)} %slice.24.refs_3_.refs_0_), channel_id=1, source_target_pairs={{0,17},{1,16},{2,19},{3,18},{4,21},{5,20},{6,23},{7,22},{8,25},{9,... | collective-permute-start | bytes 196616 | tf_op jit(solution)/shard_map/ppermute | solution.py:573
  192.1 8.2 %collective-permute-start.24 = (bf16[64,512]{1,0:T(8,128)(2,1)S(1)}, bf16[64,512]{1,0:T(8,128)(2,1)S(1)}, u32[]{:S(2)}, u32[]{:S(2)}) collective-permute-start(bf16[64,512]{1,0:T(8,128)(2,1)S(1)} %slice.24.refs_3_.refs_0_), channel_id=1, source_target_pairs={{0,16},{2,18},{4,20},{6,22},{8,24},{10,26},{12,28},{14,30},{16,0},... | collective-permute-start | bytes 196616 | tf_op jit(solution)/shard_map/ppermute | solution.py:569
  195.1 5.2 %collective-permute-start.23 = (bf16[64,512]{1,0:T(8,128)(2,1)S(1)}, bf16[64,512]{1,0:T(8,128)(2,1)S(1)}, u32[]{:S(2)}, u32[]{:S(2)}) collective-permute-start(bf16[64,512]{1,0:T(8,128)(2,1)S(1)} %slice.24.refs_3_.refs_0_), channel_id=1, source_target_pairs={{0,1},{1,0},{2,3},{3,2},{4,5},{5,4},{6,7},{7,6},{8,9},{9,8},{10,11... | collective-permute-start | bytes 196616 | tf_op jit(solution)/shard_map/ppermute | solution.py:571
  200.3 9.7 %collective-permute-start.29 = (bf16[256,512]{1,0:T(8,128)(2,1)S(1)}, bf16[256,512]{1,0:T(8,128)(2,1)S(1)}, u32[]{:S(2)}, u32[]{:S(2)}) collective-permute-start(bf16[256,512]{1,0:T(8,128)(2,1)S(1)} %join_pieces.6.refs_0_), channel_id=1, source_target_pairs={{0,12},{2,14},{4,8},{6,10},{8,4},{10,6},{12,0},{14,2},{16,28},{18,... | collective-permute-start | bytes 786440 | tf_op jit(solution)/shard_map/ppermute | solution.py:569
  201.1 11.9 %collective-permute-start.28 = (bf16[256,512]{1,0:T(8,128)(2,1)S(1)}, bf16[256,512]{1,0:T(8,128)(2,1)S(1)}, u32[]{:S(2)}, u32[]{:S(2)}) collective-permute-start(bf16[256,512]{1,0:T(8,128)(2,1)S(1)} %join_pieces.6.refs_0_), channel_id=1, source_target_pairs={{0,8},{2,10},{4,12},{6,14},{8,0},{10,2},{12,4},{14,6},{16,24},{18,... | collective-permute-start | bytes 786440 | tf_op jit(solution)/shard_map/ppermute | solution.py:569
  203.5 9.6 %collective-permute-start.27 = (bf16[256,512]{1,0:T(8,128)(2,1)S(1)}, bf16[256,512]{1,0:T(8,128)(2,1)S(1)}, u32[]{:S(2)}, u32[]{:S(2)}) collective-permute-start(bf16[256,512]{1,0:T(8,128)(2,1)S(1)} %join_pieces.6.refs_0_), channel_id=1, source_target_pairs={{0,4},{2,6},{4,0},{6,2},{8,12},{10,14},{12,8},{14,10},{16,20},{18,... | collective-permute-start | bytes 786440 | tf_op jit(solution)/shard_map/ppermute | solution.py:569
  213.1 2.7 %collective-permute-start.30 = (bf16[1024,512]{1,0:T(8,128)(2,1)S(1)}, bf16[1024,512]{1,0:T(8,128)(2,1)S(1)}, u32[]{:S(2)}, u32[]{:S(2)}) collective-permute-start(bf16[1024,512]{1,0:T(8,128)(2,1)S(1)} %join_pieces.7.refs_1_), channel_id=1, source_target_pairs={{0,2},{2,0},{4,6},{6,4},{8,10},{10,8},{12,14},{14,12},{16,18},{18,... | collective-permute-start | bytes 3145736 | tf_op jit(solution)/shard_map/ppermute | solution.py:569
where the time goes:
time: 219 us; the launch traced here: 218 us
  Pallas kernels  137 us (63%)
  waiting for transfers between devices  40.7 us (19%)
  starting transfers between devices  36.4 us (17%)
  local copies, waits for them, and re-layouts  2.64 us (1%)
    pallas_call x18, Pallas kernels, whole_call(): pl.pallas_call(wrapped, in_specs=[pl.BlockSpec(memory_space=place(k, v))...  49.3 us
    ppermute x20, waiting for transfers between devices, swapped(): lax.ppermute(block, 'dp', [(i, i ^ flips['dp']) for i in range(n_dp)])  35.5 us
    pallas_call x3, Pallas kernels, local_attention_back(): pl.pallas_call(lambda *refs: local_back_kernel(first, *refs[:9], *refs[9...  25.7 us
    ppermute x20, starting transfers between devices, swapped(): lax.ppermute(block, 'dp', [(i, i ^ flips['dp']) for i in range(n_dp)])  25.4 us
    pallas_call x1, Pallas kernels, retrieve_back(): pl.pallas_call(lambda *refs: retrieve_back_kernel(*refs[:6], *refs[6 + le...  23.1 us
    pallas_call x1, Pallas kernels, retrieve(): pl.pallas_call(retrieve_kernel, grid=(rows // count,), in_specs=[pl.Block...  16.5 us
    pallas_call x2, Pallas kernels, local_attention(): pl.pallas_call(lambda *refs: local_kernel(start, *refs[:4], *refs[4 + len...  14.8 us
    pallas_call x3, Pallas kernels, row_blocks_call(): pl.pallas_call(kernel, grid=(rows // block,), in_specs=[rows_spec(operand...  8.1 us
  transfers between devices with their start and end apart: 31, of which 15 were waited for; matrix products, arithmetic and copies ran while one was open for 0% of the time, Pallas kernels for 45%

commit v1 on v0

--- a/solution.py
+++ b/solution.py
@@ -777,10 +777,10 @@
 
 def gelu_and_slope(x):
     square = x * x
-    tanh = jnp.tanh(ROOT * (x * (1.0 + CUBE * square)))
-    half = 0.5 * (1.0 + tanh)
-    slope = half + (0.5 * ROOT) * x * (1.0 - tanh * tanh) * (1.0 + (3.0 * CUBE) * square)
-    return x * half, slope
+    half = 0.5 + 0.5 * jnp.tanh(x * (ROOT + (ROOT * CUBE) * square))
+    value = x * half
+    slope = half + (value * (1.0 - half)) * (2.0 * ROOT + (6.0 * ROOT * CUBE) * square)
+    return value, slope
 
 
 def hidden_kernel(
@@ -1178,17 +1178,17 @@
     )
     early = scatter_level(early, 2, after_far=[inner])
     steps = list(range(H // BACK_HEADS))
-    quarter = len(steps) // 4
+    first, second = len(steps) * 3 // 8, len(steps) * 5 // 8
     back = functools.partial(
         local_attention_back, base_ref, ask, halo, own, local_grad, log_total, inner, partial, far
     )
-    grads = back(steps[:quarter], after=[early[0]])
+    grads = back(steps[:first], after=[early[0]])
     early_total = scatter_finish(early, after_far=[grads[0]])
     early = gather_level(early_total, 2)
-    grads = back(steps[quarter : 2 * quarter], grads, after=[early_total])
+    grads = back(steps[first:second], grads, after=[early_total])
     early_total = join_pieces(early, after_far=[grads[0]])
     early = gather_level(early_total, 1)
-    ask_grad, memory_grad = back(steps[2 * quarter :], grads, after=[early_total])
+    ask_grad, memory_grad = back(steps[second:], grads, after=[early_total])
     own_grad, others_grad, first_gain_grad = normed_back(
         inputs, far_inputs, halo_inputs, ask_grad, memory_grad, ask_weight, memory_weight
     )
@@ -1201,7 +1201,10 @@
     early_own = join_pieces(early, after=[own_late])
     early_other = swapped(early_own, level_groups()[0][0], 1)
     late = scatter_level(late, 1, EXTRA_ROWS, after=[early_own])
-    late = scatter_level(late, 2, EXTRA_ROWS)
+    return_sum, hidden_sum, token = unpack_early(
+        chunk, early_own, early_other, return_weight.shape, hidden_weight.shape, after=[late[0]]
+    )
+    late = scatter_level(late, 2, EXTRA_ROWS, after=[token])
     input_grad, token = whole_call(
         input_back_kernel, "input_back", inputs, gain_rows(first_gain), resid_grad, own_grad, *arrived,
         outs=[((rows, width), BF16), TOKEN], after=[late[0]],
@@ -1210,10 +1213,7 @@
     extra = late_total[LATE_ROWS:]
     late_total = late_total[:LATE_ROWS]
     late = gather_level(late_total, 2)
-    return_sum, hidden_sum, token = unpack_early(
-        chunk, early_own, early_other, return_weight.shape, hidden_weight.shape, after=[late_total]
-    )
-    late_total = join_pieces(late, after=[token])
+    late_total = join_pieces(late)
     late = gather_level(late_total, 1)
     late_own = join_pieces(late)
     late_other = swapped(late_own, level_groups()[0][0], 1)

time: 219 us -> 218 us (level)
    ppermute x20, waiting for transfers between devices: 35.5 us -> 30.8 us  [swapped(): lax.ppermute(block, 'dp', [(i, i ^ flips['dp']) for i in range(n_dp)])]
    ppermute x4, waiting for transfers between devices: 5.05 us -> 9.55 us  [swapped(): return lax.ppermute(block, ('dp', 'seq'), route)]
  transfers between devices with their start and end apart: 31 -> 31, of which waited for: 15 -> 18; matrix products, arithmetic and copies ran while one was open for 0% -> 0% of each run, Pallas kernels for 45% -> 45%
where the time goes in v1:
time: 218 us; the launch traced here: 217 us
  Pallas kernels  137 us (63%)
  waiting for transfers between devices  40.4 us (19%)
  starting transfers between devices  35.8 us (16%)
  local copies, waits for them, and re-layouts  2.64 us (1%)
    pallas_call x18, Pallas kernels, whole_call(): pl.pallas_call(wrapped, in_specs=[pl.BlockSpec(memory_space=place(k, v))...  49.2 us
    ppermute x20, waiting for transfers between devices, swapped(): lax.ppermute(block, 'dp', [(i, i ^ flips['dp']) for i in range(n_dp)])  30.8 us
    pallas_call x3, Pallas kernels, local_attention_back(): pl.pallas_call(lambda *refs: local_back_kernel(first, *refs[:9], *refs[9...  25.7 us
    ppermute x20, starting transfers between devices, swapped(): lax.ppermute(block, 'dp', [(i, i ^ flips['dp']) for i in range(n_dp)])  24.1 us
    pallas_call x1, Pallas kernels, retrieve_back(): pl.pallas_call(lambda *refs: retrieve_back_kernel(*refs[:6], *refs[6 + le...  23 us
    pallas_call x1, Pallas kernels, retrieve(): pl.pallas_call(retrieve_kernel, grid=(rows // count,), in_specs=[pl.Block...  16.5 us
    pallas_call x2, Pallas kernels, local_attention(): pl.pallas_call(lambda *refs: local_kernel(start, *refs[:4], *refs[4 + len...  14.8 us
    ppermute x4, waiting for transfers between devices, swapped(): return lax.ppermute(block, ('dp', 'seq'), route)  9.55 us
  transfers between devices with their start and end apart: 31, of which 18 were waited for; matrix products, arithmetic and copies ran while one was open for 0% of the time, Pallas kernels for 45%

profile of v1, /device:TPU:0, one launch (start us, length us, event | category | flops | bytes accessed | tf_op | source)
XLA Modules:
  0.0 217.1 jit_solution(4293979763561155032)
XLA Ops:
  0.7 2.1 slice_bitcast_fusion
  2.7 2.9 %collective-permute-start.1 = (bf16[512,512]{1,0:T(8,128)(2,1)}, bf16[512,512]{1,0:T(8,128)(2,1)S(1)}, u32[]{:S(2)}, u32[]{:S(2)}) collective-permute-start(bf16[512,512]{1,0:T(8,128)(2,1)} %get-tuple-element.151), channel_id=1, source_target_pairs={{1,0},{0,1},{3,2},{2,3},{5,4},{4,5},{7,6},{6,7},{9,8},{8,9},{11,10... | collective-permute-start | bytes 1572872 | tf_op jit(solution)/shard_map/ppermute | solution.py:536
  5.8 0.2 copy.30
  6.0 0.3 add.33
  6.3 2.4 %lay_weights.1 = (bf16[512,1024]{1,0:T(8,128)(2,1)S(1)}, bf16[512,1024]{1,0:T(8,128)(2,1)S(1)}, bf16[1024,512]{1,0:T(8,128)(2,1)S(1)}) custom-call(bf16[512,512]{1,0:T(8,128)(2,1)} %refs_0_.1, bf16[512,512]{1,0:T(8,128)(2,1)} %refs_1_.1, bf16[512,512]{1,0:T(8,128)(2,1)} %refs_2_.1, bf16[8,512]{1,0:T(8,128)(2,1)S(1)} %bitcast.18, bf16[512,512]{1,0:T(8,128)(2,1)} %refs_4_.1), custom_call_target="tpu_custom_call" | custom-call | flops 300000000 | bytes 900000 | tf_op jit(solution)/shard_map/lay_weights/pallas_call | solution.py:612
  8.8 4.4 %project.1 = (bf16[1024,512]{1,0:T(8,128)(2,1)}, bf16[1024,1024]{1,0:T(8,128)(2,1)}, bf16[1024,1024]{1,0:T(8,128)(2,1)}) custom-call(bf16[1024,512]{1,0:T(8,128)(2,1)S(1)} %bitcast.15, f32[8,512]{1,0:T(8,128)S(1)} %broadcast_in_dim.4.gain_ref.refs_1_, s32[1,1024]{1,0:T(1,128)S(1)} %copy-done.8, ...), custom_call_target="tpu_custom_call" | custom-call | flops 3000000000 | bytes 9000000 | tf_op jit(solution)/shard_map/project/pallas_call | solution.py:746
  13.2 7.3 %local_attention.2 = (bf16[1024,1024]{1,0:T(8,128)(2,1)}, f32[8,1024]{1,0:T(8,128)}) custom-call(s32[1]{0:T(128)} %bitcast.6.refs_0_, bf16[1024,1024]{1,0:T(8,128)(2,1)} %get-tuple-element.86.refs_1_.ask_ref.refs_2_, bf16[1024,1024]{1,0:T(8,128)(2,1)} %get-tuple-element.85.refs_2_.refs_3_.own_ref, bf16[1024,1024]{1,0:T(8,128)(2,1)} %get-tuple-element.85.refs_2_.refs_3_.own_ref), custom_call_target="tpu_custom_call" | custom-call | flops 6400000000 | bytes 19200000 | tf_op jit(solution)/shard_map/local_attention/pallas_call | solution.py:150
  20.5 1.9 project_memory.3
  22.4 7.5 %local_attention.3 = (bf16[1024,1024]{1,0:T(8,128)(2,1)}, f32[8,1024]{1,0:T(8,128)}) custom-call(s32[1]{0:T(128)} %bitcast.6.refs_0_, bf16[1024,1024]{1,0:T(8,128)(2,1)} %get-tuple-element.86.refs_1_.ask_ref.refs_2_, bf16[512,1024]{1,0:T(8,128)(2,1)} %get-tuple-element.83.refs_2_.halo_ref, ...), custom_call_target="tpu_custom_call", output_to_operand_aliasing={{0}: (4, {}), {1}: (5, {})} | custom-call | flops 6400000000 | bytes 19200000 | tf_op jit(solution)/shard_map/local_attention/pallas_call | solution.py:150
  29.8 1.9 project_memory.2
  31.7 16.5 %retrieve.1 = (bf16[4,8192,128]{2,1,0:T(8,128)(2,1)}, bf16[4,8192,128]{2,1,0:T(8,128)(2,1)}, bf16[1024,1024]{1,0:T(8,128)(2,1)S(1)}) custom-call(s32[4096]{0:T(1024)S(1)} %add_select_fusion.index_ref.refs_0_, bf16[512,1024]{1,0:T(8,128)(2,1)} %get-tuple-element.82.far_ref, bf16[512,1024]{1,0:T(8,128)(2,1)} %get-tuple-element.83.refs_2_.halo_ref, ...), custom_call_target="tpu_custom_call" | custom-call | flops 12000000000 | bytes 36000000 | tf_op jit(solution)/shard_map/retrieve/pallas_call | solution.py:376
  48.2 17.4 %hidden_layer.1 = (f32[1024,512]{1,0:T(8,128)S(1)}, bf16[1024,2048]{1,0:T(8,128)(2,1)S(1)}, bf16[1024,2048]{1,0:T(8,128)(2,1)S(1)}, bf16[2048,512]{1,0:T(8,128)(2,1)S(1)}, bf16[2048,512]{1,0:T(8,128)(2,1)S(1)}) custom-call(s32[1]{0:T(128)} %bitcast.refs_0_, bf16[1024,512]{1,0:T(8,128)(2,1)} %bitcast.14, bf16[1024,512]{1,0:T(8,128)(2,1)} %bitcast.19, ...), custom_call_target="tpu_custom_call" | custom-call | flops 20000000000 | bytes 60000000 | tf_op jit(solution)/shard_map/hidden_layer/pallas_call | solution.py:612
  65.6 9.7 %resid_layer.1 = (bf16[1024,512]{1,0:T(8,128)(2,1)}, f32[1024,512]{1,0:T(8,128)S(1)}, bf16[1024,1024]{1,0:T(8,128)(2,1)S(1)}, f32[8,512]{1,0:T(8,128)S(1)}, bf16[1024,512]{1,0:T(8,128)(2,1)S(1)}) custom-call(f32[1024,512]{1,0:T(8,128)S(1)} %get-tuple-element.92.refs_0_, bf16[1024,512]{1,0:T(8,128)(2,1)} %bitcast.20, ...), custom_call_target="tpu_custom_call" | custom-call | flops 8000000000 | bytes 24000000 | tf_op jit(solution)/shard_map/resid_layer/pallas_call | solution.py:612
  75.3 0.5 add_pieces.6
  75.8 2.0 collective-permute-start.3
  77.8 1.6 collective-permute-start.4
  79.4 23.0 %retrieve_back.1 = (bf16[1024,1024]{1,0:T(8,128)(2,1)}, f32[8,1024]{1,0:T(8,128)}, bf16[1024,1024]{1,0:T(8,128)(2,1)}, bf16[2048,1024]{1,0:T(8,128)(2,1)}) custom-call(s32[4096]{0:T(1024)S(1)} %add_select_fusion.index_ref.refs_0_, bf16[1024,1024]{1,0:T(8,128)(2,1)S(1)} %get-tuple-element.97.refs_1_, ...), custom_call_target="tpu_custom_call" | custom-call | flops 24000000000 | bytes 72000000 | tf_op jit(solution)/shard_map/retrieve_back/pallas_call | solution.py:495
  102.4 0.4 collective-permute-done.5.refs_3_
  102.9 0.3 add_pieces.7
  103.1 1.7 collective-permute-start.6
  104.9 2.6 %collective-permute-start.7 = (bf16[128,512]{1,0:T(8,128)(2,1)S(1)}, bf16[128,512]{1,0:T(8,128)(2,1)S(1)}, u32[]{:S(2)}, u32[]{:S(2)}) collective-permute-start(bf16[128,512]{1,0:T(8,128)(2,1)S(1)} %get-tuple-element.116), channel_id=1, source_target_pairs={{0,16},{2,18},{4,20},{6,22},{8,24},{10,26},{12,28},{14,30},{16,0},... | collective-permute-start | bytes 393224 | tf_op jit(solution)/shard_map/ppermute | solution.py:569
  107.4 0.2 collective-permute-start.8
  107.6 9.3 %local_attention_back.3 = (bf16[1024,1024]{1,0:T(8,128)(2,1)}, bf16[2048,1024]{1,0:T(8,128)(2,1)}) custom-call(s32[1]{0:T(128)} %bitcast.6.refs_0_, bf16[1024,1024]{1,0:T(8,128)(2,1)} %get-tuple-element.86.refs_1_.ask_ref.refs_2_, bf16[512,1024]{1,0:T(8,128)(2,1)} %get-tuple-element.83.refs_2_.halo_ref, ...), custom_call_target="tpu_custom_call" | custom-call | flops 300000000 | bytes 900000 | tf_op jit(solution)/shard_map/local_attention_back/pallas_call | solution.py:230
  116.9 0.2 collective-permute-done.7.refs_2_
  117.1 1.7 collective-permute-done.8.refs_3_
  118.9 1.8 collective-permute-start.11
  120.7 2.0 collective-permute-start.10
  122.7 0.6 collective-permute-start.9
  123.3 7.0 %local_attention_back.4 = (bf16[1024,1024]{1,0:T(8,128)(2,1)}, bf16[2048,1024]{1,0:T(8,128)(2,1)}) custom-call(s32[1]{0:T(128)} %bitcast.6.refs_0_, bf16[1024,1024]{1,0:T(8,128)(2,1)} %get-tuple-element.86.refs_1_.ask_ref.refs_2_, bf16[512,1024]{1,0:T(8,128)(2,1)} %get-tuple-element.83.refs_2_.halo_ref, ...), custom_call_target="tpu_custom_call", output_to_operand_aliasing={{0}: (9, {}), {1}: (10, {})} | custom-call | flops 300000000 | bytes 900000 | tf_op jit(solution)/shard_map/local_attention_back/pallas_call | solution.py:230
  130.3 1.9 collective-permute-done.11.refs_3_
  132.2 1.3 collective-permute-done.10.refs_2_
  133.5 0.3 collective-permute-start.16
  133.9 2.7 %collective-permute-start.15 = (bf16[512,512]{1,0:T(8,128)(2,1)S(1)}, bf16[512,512]{1,0:T(8,128)(2,1)S(1)}, u32[]{:S(2)}, u32[]{:S(2)}) collective-permute-start(bf16[512,512]{1,0:T(8,128)(2,1)S(1)} %join_pieces.4.refs_11_.refs_0_), channel_id=1, source_target_pairs={{0,8},{2,10},{4,12},{6,14},{8,0},{10,2},{12,4},{14,6},{16,24},{18,... | collective-permute-start | bytes 1572872 | tf_op jit(solution)/shard_map/ppermute | solution.py:569
  136.6 0.5 collective-permute-start.14
  137.1 9.4 %local_attention_back.5 = (bf16[1024,1024]{1,0:T(8,128)(2,1)}, bf16[2048,1024]{1,0:T(8,128)(2,1)}) custom-call(s32[1]{0:T(128)} %bitcast.6.refs_0_, bf16[1024,1024]{1,0:T(8,128)(2,1)} %get-tuple-element.86.refs_1_.ask_ref.refs_2_, bf16[512,1024]{1,0:T(8,128)(2,1)} %get-tuple-element.83.refs_2_.halo_ref, ...), custom_call_target="tpu_custom_call", output_to_operand_aliasing={{0}: (9, {}), {1}: (10, {})} | custom-call | flops 300000000 | bytes 900000 | tf_op jit(solution)/shard_map/local_attention_back/pallas_call | solution.py:230
  146.5 6.2 %normed_back.1 = (f32[1024,512]{1,0:T(8,128)S(1)}, bf16[1024,512]{1,0:T(8,128)(2,1)S(1)}, f32[8,512]{1,0:T(8,128)S(1)}) custom-call(bf16[1024,512]{1,0:T(8,128)(2,1)S(1)} %bitcast.16, bf16[512,512]{1,0:T(8,128)(2,1)S(1)} %collective-permute-done.inputs_ref.refs_1_, bf16[512,512]{1,0:T(8,128)(2,1)S(1)} %collective-permute-done.1.inputs_ref.refs_2_, ...), custom_call_target="tpu_custom_call" | custom-call | flops 300000000 | bytes 900000 | tf_op jit(solution)/shard_map/normed_back/pallas_call | solution.py:612
  152.8 3.7 %late_weight_grads.1 = (bf16[1040,512]{1,0:T(8,128)(2,1)S(1)}, bf16[1040,512]{1,0:T(8,128)(2,1)S(1)}) custom-call(s32[1]{0:T(128)} %bitcast.refs_0_, bf16[512,512]{1,0:T(8,128)(2,1)S(1)} %copy-done.6, bf16[512,512]{1,0:T(8,128)(2,1)S(1)} %copy-done.5, bf16[1024,512]{1,0:T(8,128)(2,1)S(1)} %copy-done.4, bf16[1024,1024]{1,0:T(8,128)(2,1)S(1)} %copy-done, ...), custom_call_target="tpu_custom_call" | custom-call | flops 300000000 | bytes 900000 | tf_op jit(solution)/shard_map/late_weight_grads/pallas_call | solution.py:612
  156.5 2.1 collective-permute-done.15.refs_2_
  158.8 0.5 collective-permute-start.13
  159.3 5.2 %collective-permute-done.13.refs_1_ = bf16[1040,512]{1,0:T(8,128)(2,1)S(1)} collective-permute-done((bf16[1040,512]{1,0:T(8,128)(2,1)S(1)}, bf16[1040,512]{1,0:T(8,128)(2,1)S(1)}, u32[]{:S(2)}, u32[]{:S(2)}) %collective-permute-start.13) | collective-permute-done | bytes 1064992 | tf_op jit(solution)/shard_map/ppermute | solution.py:569
  164.5 0.2 add_pieces.9
  164.8 1.5 collective-permute-start.17
  166.2 0.4 collective-permute-start.18
  166.6 1.7 collective-permute-start.19
  168.3 3.9 %unpack_early.1 = (f32[2048,512]{1,0:T(8,128)}, f32[512,2048]{1,0:T(8,128)}, f32[8,128]{1,0:T(8,128)S(1)}) custom-call(s32[1]{0:T(128)} %bitcast.refs_0_, bf16[2048,512]{1,0:T(8,128)(2,1)S(1)} %join_pieces.5.refs_2_.refs_1_, bf16[2048,512]{1,0:T(8,128)(2,1)S(1)} %collective-permute-done.20.refs_2_, bf16[272,512]{1,0:T(8,128)(2,1)S(1)} %get-tuple-element.131.refs_3_.refs_0_), custom_call_target="tpu_custom_call" | custom-call | flops 300000000 | bytes 900000 | tf_op jit(solution)/shard_map/unpack_early/pallas_call | solution.py:612
  172.2 1.3 collective-permute-done.17.refs_1_
  173.5 2.3 %collective-permute-done.18.refs_2_ = bf16[272,512]{1,0:T(8,128)(2,1)S(1)} collective-permute-done((bf16[272,512]{1,0:T(8,128)(2,1)S(1)}, bf16[272,512]{1,0:T(8,128)(2,1)S(1)}, u32[]{:S(2)}, u32[]{:S(2)}) %collective-permute-start.18) | collective-permute-done | bytes 278560 | tf_op jit(solution)/shard_map/ppermute | solution.py:569
  175.8 4.9 %collective-permute-done.19.refs_3_ = bf16[272,512]{1,0:T(8,128)(2,1)S(1)} collective-permute-done((bf16[272,512]{1,0:T(8,128)(2,1)S(1)}, bf16[272,512]{1,0:T(8,128)(2,1)S(1)}, u32[]{:S(2)}, u32[]{:S(2)}) %collective-permute-start.19) | collective-permute-done | bytes 278560 | tf_op jit(solution)/shard_map/ppermute | solution.py:569
  180.9 2.6 %collective-permute-start.22 = (bf16[80,512]{1,0:T(8,128)(2,1)S(1)}, bf16[80,512]{1,0:T(8,128)(2,1)S(1)}, u32[]{:S(2)}, u32[]{:S(2)}) collective-permute-start(bf16[80,512]{1,0:T(8,128)(2,1)S(1)} %get-tuple-element.139), channel_id=1, source_target_pairs={{0,16},{2,18},{4,20},{6,22},{8,24},{10,26},{12,28},{14,30},{16,0},... | collective-permute-start | bytes 245768 | tf_op jit(solution)/shard_map/ppermute | solution.py:569
  183.5 1.8 collective-permute-start.23
  185.3 2.0 input_back.1
  187.4 4.3 %collective-permute-done.23.refs_3_ = bf16[80,512]{1,0:T(8,128)(2,1)S(1)} collective-permute-done((bf16[80,512]{1,0:T(8,128)(2,1)S(1)}, bf16[80,512]{1,0:T(8,128)(2,1)S(1)}, u32[]{:S(2)}, u32[]{:S(2)}) %collective-permute-start.23) | collective-permute-done | bytes 81952 | tf_op jit(solution)/shard_map/ppermute | solution.py:573
  191.8 1.9 collective-permute-start.25
  193.8 2.4 %collective-permute-start.24 = (bf16[64,512]{1,0:T(8,128)(2,1)S(1)}, bf16[64,512]{1,0:T(8,128)(2,1)S(1)}, u32[]{:S(2)}, u32[]{:S(2)}) collective-permute-start(bf16[64,512]{1,0:T(8,128)(2,1)S(1)} %slice.24.refs_0_), channel_id=1, source_target_pairs={{0,1},{1,0},{2,3},{3,2},{4,5},{5,4},{6,7},{7,6},{8,9},{9,8},{10,11... | collective-permute-start | bytes 196616 | tf_op jit(solution)/shard_map/ppermute | solution.py:571
  196.2 1.7 collective-permute-done.26.refs_3_
  197.9 0.7 collective-permute-done.25.refs_2_
  198.7 2.9 %collective-permute-start.29 = (bf16[256,512]{1,0:T(8,128)(2,1)S(1)}, bf16[256,512]{1,0:T(8,128)(2,1)S(1)}, u32[]{:S(2)}, u32[]{:S(2)}) collective-permute-start(bf16[256,512]{1,0:T(8,128)(2,1)S(1)} %join_pieces.6.refs_0_), channel_id=1, source_target_pairs={{0,12},{2,14},{4,8},{6,10},{8,4},{10,6},{12,0},{14,2},{16,28},{18,... | collective-permute-start | bytes 786440 | tf_op jit(solution)/shard_map/ppermute | solution.py:569
  201.5 0.5 collective-permute-start.28
  202.0 0.2 collective-permute-start.27
  202.2 6.7 %collective-permute-done.29.refs_3_ = bf16[256,512]{1,0:T(8,128)(2,1)S(1)} collective-permute-done((bf16[256,512]{1,0:T(8,128)(2,1)S(1)}, bf16[256,512]{1,0:T(8,128)(2,1)S(1)}, u32[]{:S(2)}, u32[]{:S(2)}) %collective-permute-start.29) | collective-permute-done | bytes 262176 | tf_op jit(solution)/shard_map/ppermute | solution.py:569
  208.9 2.4 %collective-permute-done.28.refs_2_ = bf16[256,512]{1,0:T(8,128)(2,1)S(1)} collective-permute-done((bf16[256,512]{1,0:T(8,128)(2,1)S(1)}, bf16[256,512]{1,0:T(8,128)(2,1)S(1)}, u32[]{:S(2)}, u32[]{:S(2)}) %collective-permute-start.28) | collective-permute-done | bytes 262176 | tf_op jit(solution)/shard_map/ppermute | solution.py:569
  211.2 0.7 collective-permute-done.27.refs_1_
  212.1 2.6 %collective-permute-done.30.refs_2_ = bf16[1024,512]{1,0:T(8,128)(2,1)S(1)} collective-permute-done((bf16[1024,512]{1,0:T(8,128)(2,1)S(1)}, bf16[1024,512]{1,0:T(8,128)(2,1)S(1)}, u32[]{:S(2)}, u32[]{:S(2)}) %collective-permute-start.30) | collective-permute-done | bytes 1048608 | tf_op jit(solution)/shard_map/ppermute | solution.py:569
  214.7 2.4 %unpack_late.1 = (f32[512,512]{1,0:T(8,128)}, f32[512,512]{1,0:T(8,128)}, f32[512,512]{1,0:T(8,128)}, f32[512,512]{1,0:T(8,128)}, f32[8,512]{1,0:T(8,128)}, /*index=5*/f32[1,512]{1,0:T(1,128)}, f32[1,512]{1,0:T(1,128)}) custom-call(s32[1]{0:T(128)} %bitcast.refs_0_, bf16[1024,512]{1,0:T(8,128)(2,1)S(1)} %join_pieces.7.refs_1_, ...), custom_call_target="tpu_custom_call" | custom-call | flops 300000000 | bytes 900000 | tf_op jit(solution)/shard_map/unpack_late/pallas_call | solution.py:612
  (59 shorter events, 1.1 us)
Async XLA Ops:
  0.6 5.1 %copy-start.9 = (s32[1,1024,4]{1,2,0:T(4,128)S(1)}, s32[1,1024,4]{1,2,0:T(4,128)}, u32[]{:S(2)}) copy-start(s32[1,1024,4]{1,2,0:T(4,128)} %param.15) | copy-start | bytes 49156
  0.7 5.6 %copy-start.7 = (bf16[512,8]{0,1:T(8,128)(2,1)S(1)}, bf16[512,8]{0,1:T(8,128)(2,1)}, u32[]{:S(2)}) copy-start(bf16[512,8]{0,1:T(8,128)(2,1)} %param.21) | copy-start | bytes 24580
  2.7 6.0 %copy-start.10 = (f32[512]{0:T(512)S(1)}, f32[512]{0:T(512)}, u32[]{:S(2)}) copy-start(f32[512]{0:T(512)} %param.17) | copy-start | bytes 6148
  2.7 6.0 %copy-start.2 = (bf16[1,1024,512]{2,1,0:T(8,128)(2,1)S(1)}, bf16[1,1024,512]{2,1,0:T(8,128)(2,1)}, u32[]{:S(2)}) copy-start(bf16[1,1024,512]{2,1,0:T(8,128)(2,1)} %param.13) | copy-start | bytes 3145732
  2.7 6.0 %copy-start.8 = (s32[1,1024]{1,0:T(1,128)S(1)}, s32[1,1024]{1,0:T(1,128)}, u32[]{:S(2)}) copy-start(s32[1,1024]{1,0:T(1,128)} %empty_ref.1) | copy-start | bytes 12292
  2.7 17.7 %collective-permute-start.1 = (bf16[512,512]{1,0:T(8,128)(2,1)}, bf16[512,512]{1,0:T(8,128)(2,1)S(1)}, u32[]{:S(2)}, u32[]{:S(2)}) collective-permute-start(bf16[512,512]{1,0:T(8,128)(2,1)} %get-tuple-element.151), channel_id=1, source_target_pairs={{1,0},{0,1},{3,2},{2,3},{5,4},{4,5},{7,6},{6,7},{9,8},{8,9},{11,10... | collective-permute-start | bytes 1572872 | tf_op jit(solution)/shard_map/ppermute | solution.py:536
  5.7 24.1 %collective-permute-start = (bf16[512,512]{1,0:T(8,128)(2,1)S(1)}, bf16[512,512]{1,0:T(8,128)(2,1)S(1)}, u32[]{:S(2)}, u32[]{:S(2)}) collective-permute-start(bf16[512,512]{1,0:T(8,128)(2,1)S(1)} %get-tuple-element.152), channel_id=1, source_target_pairs={{1,0},{0,1},{3,2},{2,3},{5,4},{4,5},{7,6},{6,7},{9,8},{8,9},{11,10... | collective-permute-start | bytes 1572872 | tf_op jit(solution)/shard_map/ppermute | solution.py:536
  31.7 16.5 %copy-start.11 = (f32[512]{0:T(512)S(1)}, f32[512]{0:T(512)}, u32[]{:S(2)}) copy-start(f32[512]{0:T(512)} %param.23) | copy-start | bytes 6148
  65.5 9.8 %collective-permute-start.2 = (bf16[2048,512]{1,0:T(8,128)(2,1)S(1)}, bf16[2048,512]{1,0:T(8,128)(2,1)S(1)}, u32[]{:S(2)}, u32[]{:S(2)}) collective-permute-start(bf16[2048,512]{1,0:T(8,128)(2,1)S(1)} %get-tuple-element.101), channel_id=1, source_target_pairs={{0,2},{2,0},{4,6},{6,4},{8,10},{10,8},{12,14},{14,12},{16,18},{18,... | collective-permute-start | bytes 6291464 | tf_op jit(solution)/shard_map/ppermute | solution.py:569
  75.8 26.6 %collective-permute-start.3 = (bf16[512,512]{1,0:T(8,128)(2,1)S(1)}, bf16[512,512]{1,0:T(8,128)(2,1)S(1)}, u32[]{:S(2)}, u32[]{:S(2)}) collective-permute-start(bf16[512,512]{1,0:T(8,128)(2,1)S(1)} %get-tuple-element.109), channel_id=1, source_target_pairs={{0,4},{2,6},{4,0},{6,2},{8,12},{10,14},{12,8},{14,10},{16,20},{18,... | collective-permute-start | bytes 1572872 | tf_op jit(solution)/shard_map/ppermute | solution.py:569
  77.8 24.6 %collective-permute-start.4 = (bf16[512,512]{1,0:T(8,128)(2,1)S(1)}, bf16[512,512]{1,0:T(8,128)(2,1)S(1)}, u32[]{:S(2)}, u32[]{:S(2)}) collective-permute-start(bf16[512,512]{1,0:T(8,128)(2,1)S(1)} %get-tuple-element.110), channel_id=1, source_target_pairs={{0,8},{2,10},{4,12},{6,14},{8,0},{10,2},{12,4},{14,6},{16,24},{18,... | collective-permute-start | bytes 1572872 | tf_op jit(solution)/shard_map/ppermute | solution.py:569
  79.4 23.5 %collective-permute-start.5 = (bf16[512,512]{1,0:T(8,128)(2,1)S(1)}, bf16[512,512]{1,0:T(8,128)(2,1)S(1)}, u32[]{:S(2)}, u32[]{:S(2)}) collective-permute-start(bf16[512,512]{1,0:T(8,128)(2,1)S(1)} %get-tuple-element.111), channel_id=1, source_target_pairs={{0,12},{2,14},{4,8},{6,10},{8,4},{10,6},{12,0},{14,2},{16,28},{18,... | collective-permute-start | bytes 1572872 | tf_op jit(solution)/shard_map/ppermute | solution.py:569
  103.1 13.8 %collective-permute-start.6 = (bf16[128,512]{1,0:T(8,128)(2,1)S(1)}, bf16[128,512]{1,0:T(8,128)(2,1)S(1)}, u32[]{:S(2)}, u32[]{:S(2)}) collective-permute-start(bf16[128,512]{1,0:T(8,128)(2,1)S(1)} %get-tuple-element.115), channel_id=1, source_target_pairs={{0,1},{1,0},{2,3},{3,2},{4,5},{5,4},{6,7},{7,6},{8,9},{9,8},{10,11... | collective-permute-start | bytes 393224 | tf_op jit(solution)/shard_map/ppermute | solution.py:571
  104.9 12.3 %collective-permute-start.7 = (bf16[128,512]{1,0:T(8,128)(2,1)S(1)}, bf16[128,512]{1,0:T(8,128)(2,1)S(1)}, u32[]{:S(2)}, u32[]{:S(2)}) collective-permute-start(bf16[128,512]{1,0:T(8,128)(2,1)S(1)} %get-tuple-element.116), channel_id=1, source_target_pairs={{0,16},{2,18},{4,20},{6,22},{8,24},{10,26},{12,28},{14,30},{16,0},... | collective-permute-start | bytes 393224 | tf_op jit(solution)/shard_map/ppermute | solution.py:569
  107.4 11.4 %collective-permute-start.8 = (bf16[128,512]{1,0:T(8,128)(2,1)S(1)}, bf16[128,512]{1,0:T(8,128)(2,1)S(1)}, u32[]{:S(2)}, u32[]{:S(2)}) collective-permute-start(bf16[128,512]{1,0:T(8,128)(2,1)S(1)} %get-tuple-element.117), channel_id=1, source_target_pairs={{0,17},{1,16},{2,19},{3,18},{4,21},{5,20},{6,23},{7,22},{8,25},{9,... | collective-permute-start | bytes 393224 | tf_op jit(solution)/shard_map/ppermute | solution.py:573
  118.9 13.3 %collective-permute-start.11 = (bf16[128,512]{1,0:T(8,128)(2,1)S(1)}, bf16[128,512]{1,0:T(8,128)(2,1)S(1)}, u32[]{:S(2)}, u32[]{:S(2)}) collective-permute-start(bf16[128,512]{1,0:T(8,128)(2,1)S(1)} %add_pieces.8.refs_11_.refs_0_), channel_id=1, source_target_pairs={{0,17},{1,16},{2,19},{3,18},{4,21},{5,20},{6,23},{7,22},{8,25},{9,... | collective-permute-start | bytes 393224 | tf_op jit(solution)/shard_map/ppermute | solution.py:573
  120.7 12.8 %collective-permute-start.10 = (bf16[128,512]{1,0:T(8,128)(2,1)S(1)}, bf16[128,512]{1,0:T(8,128)(2,1)S(1)}, u32[]{:S(2)}, u32[]{:S(2)}) collective-permute-start(bf16[128,512]{1,0:T(8,128)(2,1)S(1)} %add_pieces.8.refs_11_.refs_0_), channel_id=1, source_target_pairs={{0,16},{2,18},{4,20},{6,22},{8,24},{10,26},{12,28},{14,30},{16,0},... | collective-permute-start | bytes 393224 | tf_op jit(solution)/shard_map/ppermute | solution.py:569
  122.7 10.8 %collective-permute-start.9 = (bf16[128,512]{1,0:T(8,128)(2,1)S(1)}, bf16[128,512]{1,0:T(8,128)(2,1)S(1)}, u32[]{:S(2)}, u32[]{:S(2)}) collective-permute-start(bf16[128,512]{1,0:T(8,128)(2,1)S(1)} %add_pieces.8.refs_11_.refs_0_), channel_id=1, source_target_pairs={{0,1},{1,0},{2,3},{3,2},{4,5},{5,4},{6,7},{7,6},{8,9},{9,8},{10,11... | collective-permute-start | bytes 393224 | tf_op jit(solution)/shard_map/ppermute | solution.py:571
  133.5 23.0 %collective-permute-start.16 = (bf16[512,512]{1,0:T(8,128)(2,1)S(1)}, bf16[512,512]{1,0:T(8,128)(2,1)S(1)}, u32[]{:S(2)}, u32[]{:S(2)}) collective-permute-start(bf16[512,512]{1,0:T(8,128)(2,1)S(1)} %join_pieces.4.refs_11_.refs_0_), channel_id=1, source_target_pairs={{0,12},{2,14},{4,8},{6,10},{8,4},{10,6},{12,0},{14,2},{16,28},{18,... | collective-permute-start | bytes 1572872 | tf_op jit(solution)/shard_map/ppermute | solution.py:569
  133.9 24.7 %collective-permute-start.15 = (bf16[512,512]{1,0:T(8,128)(2,1)S(1)}, bf16[512,512]{1,0:T(8,128)(2,1)S(1)}, u32[]{:S(2)}, u32[]{:S(2)}) collective-permute-start(bf16[512,512]{1,0:T(8,128)(2,1)S(1)} %join_pieces.4.refs_11_.refs_0_), channel_id=1, source_target_pairs={{0,8},{2,10},{4,12},{6,14},{8,0},{10,2},{12,4},{14,6},{16,24},{18,... | collective-permute-start | bytes 1572872 | tf_op jit(solution)/shard_map/ppermute | solution.py:569
  136.6 22.0 %collective-permute-start.14 = (bf16[512,512]{1,0:T(8,128)(2,1)S(1)}, bf16[512,512]{1,0:T(8,128)(2,1)S(1)}, u32[]{:S(2)}, u32[]{:S(2)}) collective-permute-start(bf16[512,512]{1,0:T(8,128)(2,1)S(1)} %join_pieces.4.refs_11_.refs_0_), channel_id=1, source_target_pairs={{0,4},{2,6},{4,0},{6,2},{8,12},{10,14},{12,8},{14,10},{16,20},{18,... | collective-permute-start | bytes 1572872 | tf_op jit(solution)/shard_map/ppermute | solution.py:569
  137.1 9.4 %copy-start.3 = (bf16[1,1024,512]{2,1,0:T(8,128)(2,1)S(1)}, bf16[1,1024,512]{2,1,0:T(8,128)(2,1)}, u32[]{:S(2)}) copy-start(bf16[1,1024,512]{2,1,0:T(8,128)(2,1)} %param.13) | copy-start | bytes 3145732
  146.5 6.2 %copy-start = (bf16[1024,1024]{1,0:T(8,128)(2,1)S(1)}, bf16[1024,1024]{1,0:T(8,128)(2,1)}, u32[]{:S(2)}) copy-start(bf16[1024,1024]{1,0:T(8,128)(2,1)} %get-tuple-element.120.refs_3_.refs_4_) | copy-start | bytes 6291460
  146.5 6.2 %copy-start.1 = (bf16[2048,1024]{1,0:T(8,128)(2,1)S(1)}, bf16[2048,1024]{1,0:T(8,128)(2,1)}, u32[]{:S(2)}) copy-start(bf16[2048,1024]{1,0:T(8,128)(2,1)} %get-tuple-element.121.refs_4_.refs_5_) | copy-start | bytes 12582916
  146.5 6.2 %copy-start.4 = (bf16[1024,512]{1,0:T(8,128)(2,1)S(1)}, bf16[1024,512]{1,0:T(8,128)(2,1)}, u32[]{:S(2)}) copy-start(bf16[1024,512]{1,0:T(8,128)(2,1)} %get-tuple-element.126.refs_3_) | copy-start | bytes 3145732
  146.5 6.2 %copy-start.5 = (bf16[512,512]{1,0:T(8,128)(2,1)S(1)}, bf16[512,512]{1,0:T(8,128)(2,1)}, u32[]{:S(2)}) copy-start(bf16[512,512]{1,0:T(8,128)(2,1)} %get-tuple-element.125.refs_2_) | copy-start | bytes 1572868
  146.5 6.2 %copy-start.6 = (bf16[512,512]{1,0:T(8,128)(2,1)S(1)}, bf16[512,512]{1,0:T(8,128)(2,1)}, u32[]{:S(2)}) copy-start(bf16[512,512]{1,0:T(8,128)(2,1)} %get-tuple-element.124.refs_1_) | copy-start | bytes 1572868
  158.8 9.6 %collective-permute-start.20 = (bf16[2048,512]{1,0:T(8,128)(2,1)S(1)}, bf16[2048,512]{1,0:T(8,128)(2,1)S(1)}, u32[]{:S(2)}, u32[]{:S(2)}) collective-permute-start(bf16[2048,512]{1,0:T(8,128)(2,1)S(1)} %join_pieces.5.refs_2_.refs_1_), channel_id=1, source_target_pairs={{0,2},{2,0},{4,6},{6,4},{8,10},{10,8},{12,14},{14,12},{16,18},{18,... | collective-permute-start | bytes 6291464 | tf_op jit(solution)/shard_map/ppermute | solution.py:569
  158.8 5.7 %collective-permute-start.13 = (bf16[1040,512]{1,0:T(8,128)(2,1)S(1)}, bf16[1040,512]{1,0:T(8,128)(2,1)S(1)}, u32[]{:S(2)}, u32[]{:S(2)}) collective-permute-start(bf16[1040,512]{1,0:T(8,128)(2,1)S(1)} %get-tuple-element.130), channel_id=1, source_target_pairs={{0,2},{2,0},{4,6},{6,4},{8,10},{10,8},{12,14},{14,12},{16,18},{18,... | collective-permute-start | bytes 3194888 | tf_op jit(solution)/shard_map/ppermute | solution.py:569
  159.3 26.0 %collective-permute-start.12 = (bf16[1024,512]{1,0:T(8,128)(2,1)S(1)}, bf16[1024,512]{1,0:T(8,128)(2,1)S(1)}, u32[]{:S(2)}, u32[]{:S(2)}) collective-permute-start(bf16[1024,512]{1,0:T(8,128)(2,1)S(1)} %get-tuple-element.123), channel_id=1, source_target_pairs={{1,0},{0,1},{3,2},{2,3},{5,4},{4,5},{7,6},{6,7},{9,8},{8,9},{11,10... | collective-permute-start | bytes 3145736 | tf_op jit(solution)/shard_map/ppermute | solution.py:536
  164.8 8.8 %collective-permute-start.17 = (bf16[272,512]{1,0:T(8,128)(2,1)S(1)}, bf16[272,512]{1,0:T(8,128)(2,1)S(1)}, u32[]{:S(2)}, u32[]{:S(2)}) collective-permute-start(bf16[272,512]{1,0:T(8,128)(2,1)S(1)} %get-tuple-element.132), channel_id=1, source_target_pairs={{0,4},{2,6},{4,0},{6,2},{8,12},{10,14},{12,8},{14,10},{16,20},{18,... | collective-permute-start | bytes 835592 | tf_op jit(solution)/shard_map/ppermute | solution.py:569
  166.2 9.5 %collective-permute-start.18 = (bf16[272,512]{1,0:T(8,128)(2,1)S(1)}, bf16[272,512]{1,0:T(8,128)(2,1)S(1)}, u32[]{:S(2)}, u32[]{:S(2)}) collective-permute-start(bf16[272,512]{1,0:T(8,128)(2,1)S(1)} %get-tuple-element.133), channel_id=1, source_target_pairs={{0,8},{2,10},{4,12},{6,14},{8,0},{10,2},{12,4},{14,6},{16,24},{18,... | collective-permute-start | bytes 835592 | tf_op jit(solution)/shard_map/ppermute | solution.py:569
  166.6 14.0 %collective-permute-start.19 = (bf16[272,512]{1,0:T(8,128)(2,1)S(1)}, bf16[272,512]{1,0:T(8,128)(2,1)S(1)}, u32[]{:S(2)}, u32[]{:S(2)}) collective-permute-start(bf16[272,512]{1,0:T(8,128)(2,1)S(1)} %get-tuple-element.134), channel_id=1, source_target_pairs={{0,12},{2,14},{4,8},{6,10},{8,4},{10,6},{12,0},{14,2},{16,28},{18,... | collective-permute-start | bytes 835592 | tf_op jit(solution)/shard_map/ppermute | solution.py:569
  180.8 6.6 %collective-permute-start.21 = (bf16[80,512]{1,0:T(8,128)(2,1)S(1)}, bf16[80,512]{1,0:T(8,128)(2,1)S(1)}, u32[]{:S(2)}, u32[]{:S(2)}) collective-permute-start(bf16[80,512]{1,0:T(8,128)(2,1)S(1)} %get-tuple-element.138), channel_id=1, source_target_pairs={{0,1},{1,0},{2,3},{3,2},{4,5},{5,4},{6,7},{7,6},{8,9},{9,8},{10,11... | collective-permute-start | bytes 245768 | tf_op jit(solution)/shard_map/ppermute | solution.py:571
  180.9 6.5 %collective-permute-start.22 = (bf16[80,512]{1,0:T(8,128)(2,1)S(1)}, bf16[80,512]{1,0:T(8,128)(2,1)S(1)}, u32[]{:S(2)}, u32[]{:S(2)}) collective-permute-start(bf16[80,512]{1,0:T(8,128)(2,1)S(1)} %get-tuple-element.139), channel_id=1, source_target_pairs={{0,16},{2,18},{4,20},{6,22},{8,24},{10,26},{12,28},{14,30},{16,0},... | collective-permute-start | bytes 245768 | tf_op jit(solution)/shard_map/ppermute | solution.py:569
  183.5 8.2 %collective-permute-start.23 = (bf16[80,512]{1,0:T(8,128)(2,1)S(1)}, bf16[80,512]{1,0:T(8,128)(2,1)S(1)}, u32[]{:S(2)}, u32[]{:S(2)}) collective-permute-start(bf16[80,512]{1,0:T(8,128)(2,1)S(1)} %get-tuple-element.140), channel_id=1, source_target_pairs={{0,17},{1,16},{2,19},{3,18},{4,21},{5,20},{6,23},{7,22},{8,25},{9,... | collective-permute-start | bytes 245768 | tf_op jit(solution)/shard_map/ppermute | solution.py:573
  191.7 6.2 %collective-permute-start.26 = (bf16[64,512]{1,0:T(8,128)(2,1)S(1)}, bf16[64,512]{1,0:T(8,128)(2,1)S(1)}, u32[]{:S(2)}, u32[]{:S(2)}) collective-permute-start(bf16[64,512]{1,0:T(8,128)(2,1)S(1)} %slice.24.refs_0_), channel_id=1, source_target_pairs={{0,17},{1,16},{2,19},{3,18},{4,21},{5,20},{6,23},{7,22},{8,25},{9,... | collective-permute-start | bytes 196616 | tf_op jit(solution)/shard_map/ppermute | solution.py:573
  191.8 6.8 %collective-permute-start.25 = (bf16[64,512]{1,0:T(8,128)(2,1)S(1)}, bf16[64,512]{1,0:T(8,128)(2,1)S(1)}, u32[]{:S(2)}, u32[]{:S(2)}) collective-permute-start(bf16[64,512]{1,0:T(8,128)(2,1)S(1)} %slice.24.refs_0_), channel_id=1, source_target_pairs={{0,16},{2,18},{4,20},{6,22},{8,24},{10,26},{12,28},{14,30},{16,0},... | collective-permute-start | bytes 196616 | tf_op jit(solution)/shard_map/ppermute | solution.py:569
  193.8 4.9 %collective-permute-start.24 = (bf16[64,512]{1,0:T(8,128)(2,1)S(1)}, bf16[64,512]{1,0:T(8,128)(2,1)S(1)}, u32[]{:S(2)}, u32[]{:S(2)}) collective-permute-start(bf16[64,512]{1,0:T(8,128)(2,1)S(1)} %slice.24.refs_0_), channel_id=1, source_target_pairs={{0,1},{1,0},{2,3},{3,2},{4,5},{5,4},{6,7},{7,6},{8,9},{9,8},{10,11... | collective-permute-start | bytes 196616 | tf_op jit(solution)/shard_map/ppermute | solution.py:571
  198.7 10.2 %collective-permute-start.29 = (bf16[256,512]{1,0:T(8,128)(2,1)S(1)}, bf16[256,512]{1,0:T(8,128)(2,1)S(1)}, u32[]{:S(2)}, u32[]{:S(2)}) collective-permute-start(bf16[256,512]{1,0:T(8,128)(2,1)S(1)} %join_pieces.6.refs_0_), channel_id=1, source_target_pairs={{0,12},{2,14},{4,8},{6,10},{8,4},{10,6},{12,0},{14,2},{16,28},{18,... | collective-permute-start | bytes 786440 | tf_op jit(solution)/shard_map/ppermute | solution.py:569
  201.5 9.7 %collective-permute-start.28 = (bf16[256,512]{1,0:T(8,128)(2,1)S(1)}, bf16[256,512]{1,0:T(8,128)(2,1)S(1)}, u32[]{:S(2)}, u32[]{:S(2)}) collective-permute-start(bf16[256,512]{1,0:T(8,128)(2,1)S(1)} %join_pieces.6.refs_0_), channel_id=1, source_target_pairs={{0,8},{2,10},{4,12},{6,14},{8,0},{10,2},{12,4},{14,6},{16,24},{18,... | collective-permute-start | bytes 786440 | tf_op jit(solution)/shard_map/ppermute | solution.py:569
  202.0 9.9 %collective-permute-start.27 = (bf16[256,512]{1,0:T(8,128)(2,1)S(1)}, bf16[256,512]{1,0:T(8,128)(2,1)S(1)}, u32[]{:S(2)}, u32[]{:S(2)}) collective-permute-start(bf16[256,512]{1,0:T(8,128)(2,1)S(1)} %join_pieces.6.refs_0_), channel_id=1, source_target_pairs={{0,4},{2,6},{4,0},{6,2},{8,12},{10,14},{12,8},{14,10},{16,20},{18,... | collective-permute-start | bytes 786440 | tf_op jit(solution)/shard_map/ppermute | solution.py:569
  212.0 2.7 %collective-permute-start.30 = (bf16[1024,512]{1,0:T(8,128)(2,1)S(1)}, bf16[1024,512]{1,0:T(8,128)(2,1)S(1)}, u32[]{:S(2)}, u32[]{:S(2)}) collective-permute-start(bf16[1024,512]{1,0:T(8,128)(2,1)S(1)} %join_pieces.7.refs_1_), channel_id=1, source_target_pairs={{0,2},{2,0},{4,6},{6,4},{8,10},{10,8},{12,14},{14,12},{16,18},{18,... | collective-permute-start | bytes 3145736 | tf_op jit(solution)/shard_map/ppermute | solution.py:569
